TPU v7x, 1024 devices: a whole 4x8x16 slice. The times are simulated.
1024 devices in a mesh: sites: 1024 (over x, y, z, core).
Axes of the slice: x: 4, y: 8, z: 16, core: 2. Of those that a mesh axis runs over, the one named last changes fastest.
Arguments:
- coords: float32 [8, 1572864], P(None, 'sites'), may hold values from -6 to 6
- inv_scale: float32 [8], replicated, may hold values from 0.25 to 1
- noise_var: float32 [1572864], P('sites'), may hold values from 0.5 to 2
- solution: float32 [16, 1572864], P(None, 'sites'), may hold values from -6 to 6
- residual: float32 [16, 1572864], P(None, 'sites'), may hold values from -40 to 40
- direction: float32 [16, 1572864], P(None, 'sites'), may hold values from -40 to 40
Outputs:
- new_solution: float32 [16, 1572864], P(None, 'sites')
- new_residual: float32 [16, 1572864], P(None, 'sites')
- new_direction: float32 [16, 1572864], P(None, 'sites')
All inputs are finite; a program needn't handle non-finite values.
Results may differ from a plain program's by a relative error of at most 0.0003.
Values sent between devices are 32-bit elements; how exact they have to be, the bound alone decides.
No kernel may reach another device: no remote copies, remote signals or barrier semaphores. Data moves between devices by JAX's collectives and lax.ppermute only.
A program may use at most 32 MiB of HBM per device.

v0:
```python
import jax
import jax.numpy as jnp
from jax import lax
from jax.sharding import PartitionSpec as P

ROUNDS = 3


def shifted(value, axis, steps):
    count = lax.axis_size(axis)
    pairs = [(source, (source + steps) % count) for source in range(count)]
    return lax.ppermute(value, axis, pairs)


def kernel_tile(left, right, inv_scale):
    left_scaled = left * inv_scale[:, None]
    right_scaled = right * inv_scale[:, None]
    left_norm = jnp.sum(left_scaled * left_scaled, axis=0)
    right_norm = jnp.sum(right_scaled * right_scaled, axis=0)
    cross = jnp.dot(left_scaled.T, right_scaled, precision=lax.Precision.HIGHEST)
    squared = jnp.maximum(left_norm[:, None] + right_norm[None, :] - 2.0 * cross, 0.0)
    scaled_dist = jnp.sqrt(5.0 * squared)
    return (1.0 + scaled_dist + scaled_dist * scaled_dist / 3.0) * jnp.exp(-scaled_dist)


def sweep_tile(own_coords, own_dir, far_coords, far_dir, inv_scale, with_return):
    site_count = own_coords.shape[1]
    block_rows = min(256, site_count)
    block_count = site_count // block_rows
    coord_blocks = jnp.moveaxis(
        own_coords.reshape(own_coords.shape[0], block_count, block_rows), 1, 0
    )
    dir_blocks = jnp.moveaxis(own_dir.reshape(own_dir.shape[0], block_count, block_rows), 1, 0)

    def visit_block(carried, members):
        coord_piece, dir_piece = members
        values = kernel_tile(coord_piece, far_coords, inv_scale)
        near_part = jnp.dot(far_dir, values.T, precision=lax.Precision.HIGHEST)
        if with_return:
            carried = carried + jnp.dot(dir_piece, values, precision=lax.Precision.HIGHEST)
        return (carried, near_part)

    initial = jnp.zeros(far_dir.shape, jnp.float32)
    returned, near_pieces = lax.scan(visit_block, initial, (coord_blocks, dir_blocks))
    near_total = jnp.moveaxis(near_pieces, 0, 1).reshape(own_dir.shape)
    return (near_total, returned)


def local(coords, inv_scale, noise_var, solution, residual, direction):
    self_part, unused_part = sweep_tile(coords, direction, coords, direction, inv_scale, False)
    gp_image = 2.0 * ROUNDS * self_part
    for offset in range(1, ROUNDS + 1):
        far_coords, far_dir = shifted((coords, direction), "sites", offset)
        near_total, back_total = sweep_tile(coords, direction, far_coords, far_dir, inv_scale, True)
        gp_image = gp_image + near_total
        gp_image = gp_image + shifted(back_total, "sites", -offset)
    gp_image = gp_image + noise_var[None, :] * direction
    old_norm = lax.psum(jnp.sum(residual * residual, axis=1), "sites")
    curvature = lax.psum(jnp.sum(direction * gp_image, axis=1), "sites")
    step_size = old_norm / curvature
    new_solution = solution + step_size[:, None] * direction
    new_residual = residual - step_size[:, None] * gp_image
    new_norm = lax.psum(jnp.sum(new_residual * new_residual, axis=1), "sites")
    new_direction = new_residual + (new_norm / old_norm)[:, None] * direction
    return (new_solution, new_residual, new_direction)


def solution(mesh):
    return jax.shard_map(
        local,
        mesh=mesh,
        in_specs=(
            P(None, "sites"),
            P(),
            P("sites"),
            P(None, "sites"),
            P(None, "sites"),
            P(None, "sites"),
        ),
        out_specs=(P(None, "sites"), P(None, "sites"), P(None, "sites")),
        check_vma=False,
    )
```

profile of v0, /device:TPU:1, one launch (start us, length us, event | category | flops | bytes accessed | tf_op | source)
XLA Modules:
  0.0 451.1 jit_solution(4227123721465635174)
XLA Ops:
  0.6 5.4 %collective-permute-start.1 = (f32[16,1536]{1,0:T(8,128)}, f32[16,1536]{1,0:T(8,128)S(1)}, u32[]{:S(2)}, u32[]{:S(2)}) collective-permute-start(f32[16,1536]{1,0:T(8,128)} %param.19), channel_id=1, source_target_pairs={{0,1},{1,2},{2,3},{3,4},{4,5},{5,6},{6,7},{7,8},{8,9},{9,10},{10,1... | collective-permute-start | bytes 294920 | tf_op jit(solution)/shard_map/ppermute | solution.py:12
  6.0 4.0 collective-permute-start.4
  12.3 4.0 collective-permute-start.3
  16.3 7.4 %collective-permute-start.7 = (f32[16,1536]{1,0:T(8,128)}, f32[16,1536]{1,0:T(8,128)S(1)}, u32[]{:S(2)}, u32[]{:S(2)}) collective-permute-start(f32[16,1536]{1,0:T(8,128)} %param.19), channel_id=1, source_target_pairs={{0,3},{1,4},{2,5},{3,6},{4,7},{5,8},{6,9},{7,10},{8,11},{9,12},{10... | collective-permute-start | bytes 294920 | tf_op jit(solution)/shard_map/ppermute | solution.py:12
  23.7 37.7 %while.49 = (s32[]{:T(128)}, f32[6,16,256]{2,1,0:T(8,128)S(1)}, f32[6,8,256]{2,1,0:T(8,128)}, f32[8]{0:T(128)}, f32[8,1536]{1,0:T(8,128)}, /*index=5*/f32[16,1536]{1,0:T(8,128)}, s32[]{:T(128)}) while((s32[]{:T(128)}, f32[6,16,256]{2,1,0:T(8,128)S(1)}, f32[6,8,256]{2,1,0:T(8,128)}, f32[8]{0:T(128)}, f32[8,1536]{1,0:T(8,128)}, ...), condition=%wide.region_5.6_spmd, body=%wide.region_2.5_spmd.sunk | while | flops 117627136 | bytes 3784369 | solution.py:44
  62.6 3.9 collective-permute-start.6
  66.5 41.2 %while.50 = (s32[]{:T(128)}, f32[16,1536]{1,0:T(8,128)S(1)}, f32[6,16,256]{2,1,0:T(8,128)S(1)}, f32[6,16,256]{2,1,0:T(8,128)S(1)}, f32[6,8,256]{2,1,0:T(8,128)},...) while((s32[]{:T(128)}, f32[16,1536]{1,0:T(8,128)S(1)}, ...), condition=%wide.region_9.10_spmd.clone, body=%wide.region_6.0_spmd.clone.sunk | while | flops 193173760 | bytes 5177019 | solution.py:44
  68.0 3.1 exponential_multiply_fusion.6
  74.9 3.1 exponential_multiply_fusion.6
  81.8 3.1 exponential_multiply_fusion.6
  88.7 3.1 exponential_multiply_fusion.6
  95.5 3.1 exponential_multiply_fusion.6
  102.4 3.1 exponential_multiply_fusion.6
  110.2 41.2 %while.51 = (s32[]{:T(128)}, f32[16,1536]{1,0:T(8,128)S(1)}, f32[6,16,256]{2,1,0:T(8,128)S(1)}, f32[6,16,256]{2,1,0:T(8,128)S(1)}, f32[6,8,256]{2,1,0:T(8,128)},...) while((s32[]{:T(128)}, f32[16,1536]{1,0:T(8,128)S(1)}, ...), condition=%wide.region_13.14_spmd.clone, body=%wide.region_10.0_spmd.clone.sunk | while | flops 193173760 | bytes 5177019 | solution.py:44
  111.7 3.1 exponential_multiply_fusion.7
  118.6 3.1 exponential_multiply_fusion.7
  125.5 3.1 exponential_multiply_fusion.7
  132.3 3.1 exponential_multiply_fusion.7
  139.2 3.1 exponential_multiply_fusion.7
  146.1 3.1 exponential_multiply_fusion.7
  151.4 8.9 %collective-permute-start.5 = (f32[16,1536]{1,0:T(8,128)S(1)}, f32[16,1536]{1,0:T(8,128)S(1)}, u32[]{:S(2)}, u32[]{:S(2)}) collective-permute-start(f32[16,1536]{1,0:T(8,128)S(1)} %get-tuple-element.168), channel_id=1, source_target_pairs={{0,1022},{1,1023},{2,0},{3,1},{4,2},{5,3},{6,4},{7,5},{8,6},{9,7},... | collective-permute-start | bytes 294920 | tf_op jit(solution)/shard_map/ppermute | solution.py:12
  160.4 41.3 %while.52 = (s32[]{:T(128)}, f32[16,1536]{1,0:T(8,128)S(1)}, f32[6,16,256]{2,1,0:T(8,128)S(1)}, f32[6,16,256]{2,1,0:T(8,128)S(1)}, f32[6,8,256]{2,1,0:T(8,128)},...) while((s32[]{:T(128)}, f32[16,1536]{1,0:T(8,128)S(1)}, ...), condition=%wide.region_17.18_spmd.clone, body=%wide.region_14.0_spmd.clone.sunk | while | flops 193173760 | bytes 5177019 | solution.py:44
  161.9 3.1 exponential_multiply_fusion.8
  168.8 3.1 exponential_multiply_fusion.8
  175.7 3.1 exponential_multiply_fusion.8
  182.5 3.1 exponential_multiply_fusion.8
  189.4 3.1 exponential_multiply_fusion.8
  196.3 3.1 exponential_multiply_fusion.8
  201.6 5.7 %collective-permute-start.8 = (f32[16,1536]{1,0:T(8,128)S(1)}, f32[16,1536]{1,0:T(8,128)S(1)}, u32[]{:S(2)}, u32[]{:S(2)}) collective-permute-start(f32[16,1536]{1,0:T(8,128)S(1)} %get-tuple-element.170), channel_id=1, source_target_pairs={{0,1021},{1,1022},{2,1023},{3,0},{4,1},{5,2},{6,3},{7,4},{8,5},{9,... | collective-permute-start | bytes 294920 | tf_op jit(solution)/shard_map/ppermute | solution.py:12
  207.4 3.2 collective-permute-done.8
  210.8 122.0 %all-reduce = (f32[16]{0:T(128)S(1)}, f32[16]{0:T(128)S(1)}) all-reduce(f32[16]{0:T(128)S(1)} %multiply_reduce_fusion.10, f32[16]{0:T(128)S(1)} %get-tuple-element.340), channel_id=1, replica_groups=mesh['sites'=1024] {'sites'}, use_global_device_ids=true, to_apply=%region_1.0 | all-reduce | flops 32 | bytes 256 | tf_op jit(solution)/shard_map/psum | solution.py:58
  333.0 117.3 %psum.23 = f32[16]{0:T(128)S(1)} all-reduce(f32[16]{0:T(128)S(1)} %get-tuple-element.338), channel_id=1, replica_groups=mesh['sites'=1024] {'sites'}, use_global_device_ids=true, to_apply=%region_21.22 | all-reduce | flops 16 | bytes 128 | tf_op jit(solution)/shard_map/psum | solution.py:63
  (147 shorter events, 111.5 us)
Async XLA Ops:
  0.6 65.8 %collective-permute-start.1 = (f32[16,1536]{1,0:T(8,128)}, f32[16,1536]{1,0:T(8,128)S(1)}, u32[]{:S(2)}, u32[]{:S(2)}) collective-permute-start(f32[16,1536]{1,0:T(8,128)} %param.19), channel_id=1, source_target_pairs={{0,1},{1,2},{2,3},{3,4},{4,5},{5,6},{6,7},{7,8},{8,9},{9,10},{10,1... | collective-permute-start | bytes 294920 | tf_op jit(solution)/shard_map/ppermute | solution.py:12
  6.0 104.1 %collective-permute-start.4 = (f32[16,1536]{1,0:T(8,128)}, f32[16,1536]{1,0:T(8,128)S(1)}, u32[]{:S(2)}, u32[]{:S(2)}) collective-permute-start(f32[16,1536]{1,0:T(8,128)} %param.19), channel_id=1, source_target_pairs={{0,2},{1,3},{2,4},{3,5},{4,6},{5,7},{6,8},{7,9},{8,10},{9,11},{10,... | collective-permute-start | bytes 294920 | tf_op jit(solution)/shard_map/ppermute | solution.py:12
  10.0 52.5 %collective-permute-start = (f32[8,1536]{1,0:T(8,128)}, f32[8,1536]{1,0:T(8,128)S(1)}, u32[]{:S(2)}, u32[]{:S(2)}) collective-permute-start(f32[8,1536]{1,0:T(8,128)} %param.14), channel_id=1, source_target_pairs={{0,1},{1,2},{2,3},{3,4},{4,5},{5,6},{6,7},{7,8},{8,9},{9,10},{10,1... | collective-permute-start | bytes 147464 | tf_op jit(solution)/shard_map/ppermute | solution.py:12
  12.3 97.9 %collective-permute-start.3 = (f32[8,1536]{1,0:T(8,128)}, f32[8,1536]{1,0:T(8,128)S(1)}, u32[]{:S(2)}, u32[]{:S(2)}) collective-permute-start(f32[8,1536]{1,0:T(8,128)} %param.14), channel_id=1, source_target_pairs={{0,2},{1,3},{2,4},{3,5},{4,6},{5,7},{6,8},{7,9},{8,10},{9,11},{10,... | collective-permute-start | bytes 147464 | tf_op jit(solution)/shard_map/ppermute | solution.py:12
  16.3 144.0 %collective-permute-start.7 = (f32[16,1536]{1,0:T(8,128)}, f32[16,1536]{1,0:T(8,128)S(1)}, u32[]{:S(2)}, u32[]{:S(2)}) collective-permute-start(f32[16,1536]{1,0:T(8,128)} %param.19), channel_id=1, source_target_pairs={{0,3},{1,4},{2,5},{3,6},{4,7},{5,8},{6,9},{7,10},{8,11},{9,12},{10... | collective-permute-start | bytes 294920 | tf_op jit(solution)/shard_map/ppermute | solution.py:12
  23.7 37.7 %copy-start.2 = (f32[16,1536]{1,0:T(8,128)S(1)}, f32[16,1536]{1,0:T(8,128)}, u32[]{:S(2)}) copy-start(f32[16,1536]{1,0:T(8,128)} %param.18) | copy-start | bytes 294916
  23.7 4.7 %copy-start = (f32[16,1536]{1,0:T(8,128)S(1)}, f32[16,1536]{1,0:T(8,128)}, u32[]{:S(2)}) copy-start(f32[16,1536]{1,0:T(8,128)} %get-tuple-element.637) | copy-start | bytes 294916 | tf_op jit(solution)/shard_map/while
  30.0 4.7 %copy-start = (f32[16,1536]{1,0:T(8,128)S(1)}, f32[16,1536]{1,0:T(8,128)}, u32[]{:S(2)}) copy-start(f32[16,1536]{1,0:T(8,128)} %get-tuple-element.637) | copy-start | bytes 294916 | tf_op jit(solution)/shard_map/while
  36.3 4.7 %copy-start = (f32[16,1536]{1,0:T(8,128)S(1)}, f32[16,1536]{1,0:T(8,128)}, u32[]{:S(2)}) copy-start(f32[16,1536]{1,0:T(8,128)} %get-tuple-element.637) | copy-start | bytes 294916 | tf_op jit(solution)/shard_map/while
  42.6 4.7 %copy-start = (f32[16,1536]{1,0:T(8,128)S(1)}, f32[16,1536]{1,0:T(8,128)}, u32[]{:S(2)}) copy-start(f32[16,1536]{1,0:T(8,128)} %get-tuple-element.637) | copy-start | bytes 294916 | tf_op jit(solution)/shard_map/while
  48.8 4.7 %copy-start = (f32[16,1536]{1,0:T(8,128)S(1)}, f32[16,1536]{1,0:T(8,128)}, u32[]{:S(2)}) copy-start(f32[16,1536]{1,0:T(8,128)} %get-tuple-element.637) | copy-start | bytes 294916 | tf_op jit(solution)/shard_map/while
  55.1 4.7 %copy-start = (f32[16,1536]{1,0:T(8,128)S(1)}, f32[16,1536]{1,0:T(8,128)}, u32[]{:S(2)}) copy-start(f32[16,1536]{1,0:T(8,128)} %get-tuple-element.637) | copy-start | bytes 294916 | tf_op jit(solution)/shard_map/while
  62.6 97.7 %collective-permute-start.6 = (f32[8,1536]{1,0:T(8,128)}, f32[8,1536]{1,0:T(8,128)S(1)}, u32[]{:S(2)}, u32[]{:S(2)}) collective-permute-start(f32[8,1536]{1,0:T(8,128)} %get-tuple-element.641), channel_id=1, source_target_pairs={{0,3},{1,4},{2,5},{3,6},{4,7},{5,8},{6,9},{7,10},{8,11},{9,12},{10... | collective-permute-start | bytes 147464 | tf_op jit(solution)/shard_map/ppermute | solution.py:12
  107.7 99.7 %collective-permute-start.2 = (f32[16,1536]{1,0:T(8,128)S(1)}, f32[16,1536]{1,0:T(8,128)S(1)}, u32[]{:S(2)}, u32[]{:S(2)}) collective-permute-start(f32[16,1536]{1,0:T(8,128)S(1)} %get-tuple-element.166), channel_id=1, source_target_pairs={{0,1023},{1,0},{2,1},{3,2},{4,3},{5,4},{6,5},{7,6},{8,7},{9,8},{10... | collective-permute-start | bytes 294920 | tf_op jit(solution)/shard_map/ppermute | solution.py:12
  151.4 56.0 %collective-permute-start.5 = (f32[16,1536]{1,0:T(8,128)S(1)}, f32[16,1536]{1,0:T(8,128)S(1)}, u32[]{:S(2)}, u32[]{:S(2)}) collective-permute-start(f32[16,1536]{1,0:T(8,128)S(1)} %get-tuple-element.168), channel_id=1, source_target_pairs={{0,1022},{1,1023},{2,0},{3,1},{4,2},{5,3},{6,4},{7,5},{8,6},{9,7},... | collective-permute-start | bytes 294920 | tf_op jit(solution)/shard_map/ppermute | solution.py:12
  160.3 50.3 %copy-start.1 = (f32[16,1536]{1,0:T(8,128)S(1)}, f32[16,1536]{1,0:T(8,128)}, u32[]{:S(2)}) copy-start(f32[16,1536]{1,0:T(8,128)} %get-tuple-element.659) | copy-start | bytes 294916
  160.3 50.3 %copy-start.5 = (f32[1536]{0:T(1024)S(1)}, f32[1536]{0:T(1024)}, u32[]{:S(2)}) copy-start(f32[1536]{0:T(1024)} %param.16) | copy-start | bytes 18436
  201.6 248.7 %copy-start.4 = (f32[16,1536]{1,0:T(8,128)S(1)}, f32[16,1536]{1,0:T(8,128)}, u32[]{:S(2)}) copy-start(f32[16,1536]{1,0:T(8,128)} %param.17) | copy-start | bytes 294916
  201.6 9.0 %collective-permute-start.8 = (f32[16,1536]{1,0:T(8,128)S(1)}, f32[16,1536]{1,0:T(8,128)S(1)}, u32[]{:S(2)}, u32[]{:S(2)}) collective-permute-start(f32[16,1536]{1,0:T(8,128)S(1)} %get-tuple-element.170), channel_id=1, source_target_pairs={{0,1021},{1,1022},{2,1023},{3,0},{4,1},{5,2},{6,3},{7,4},{8,5},{9,... | collective-permute-start | bytes 294920 | tf_op jit(solution)/shard_map/ppermute | solution.py:12
  333.0 118.1 %copy-start.3 = (f32[16,1536]{1,0:T(8,128)}, f32[16,1536]{1,0:T(8,128)S(1)}, u32[]{:S(2)}) copy-start(f32[16,1536]{1,0:T(8,128)S(1)} %get-tuple-element.339) | copy-start | bytes 294916
where the time goes:
time: 454 us; the launch traced here: 451 us
  blocking collectives  239 us (53%)
  matrix products  123 us (27%)
  starting transfers between devices  43.9 us (10%)
  other arithmetic  39.3 us (9%)
    psum x1, blocking collectives, local(): old_norm = lax.psum(jnp.sum(residual * residual, axis=1), 'sites')  122 us
    psum x1, blocking collectives, local(): new_norm = lax.psum(jnp.sum(new_residual * new_residual, axis=1), 'sites')  117 us
    dot_general x24, matrix products, kernel_tile(): jnp.dot(left_scaled.T, right_scaled, precision=lax.Precision.HIGHEST)  74.1 us
    ppermute x9, starting transfers between devices, shifted(): return lax.ppermute(value, axis, pairs)  43.9 us
    dot_general x24, matrix products, visit_block(): near_part = jnp.dot(far_dir, values.T, precision=lax.Precision.HIGHEST)  33.3 us
    reduce_sum x24, other arithmetic, kernel_tile(): left_norm = jnp.sum(left_scaled * left_scaled, axis=0)  19.3 us
    reduce_sum x24, other arithmetic, kernel_tile(): right_norm = jnp.sum(right_scaled * right_scaled, axis=0)  18.7 us
    dot_general x18, matrix products, visit_block(): jnp.dot(dir_piece, values, precision=lax.Precision.HIGHEST)  15.5 us
  transfers between devices with their start and end apart: 9, of which 1 were waited for; matrix products, arithmetic and copies ran while one was open for 36% of the time, Pallas kernels for 0%

commit v1 on v0

v1 whole, which is shorter than its diff:
```python
import functools
import math

import jax
import jax.numpy as jnp
from jax import lax
from jax.experimental import pallas as pl
from jax.experimental.pallas import tpu as pltpu
from jax.sharding import Mesh, PartitionSpec as P

ROUNDS = 3
TILE = 256
AXES = ("hi", "lo")
VMEM_LIMIT = 40 * 1024 * 1024

LN2 = math.log(2.0)
COORD_SCALE = math.sqrt(5.0) / LN2
SCALE = LN2 * LN2 / 3.0
LINEAR = 3.0 / LN2
CONSTANT = 1.0 / SCALE
TINY = 1e-30

bf16 = jnp.bfloat16
f32 = jnp.float32


def split2(value):
    high = value.astype(bf16)
    return high, (value - high.astype(f32)).astype(bf16)


def split3(value):
    high = value.astype(bf16).astype(f32)
    rest = value - high
    middle = rest.astype(bf16).astype(f32)
    low = (rest - middle).astype(bf16).astype(f32)
    return high, middle, low


def stacked(value):
    return jnp.concatenate(split2(value), axis=0)


def features(scaled, left):
    high, middle, low = split3(-2.0 * scaled if left else scaled)
    norm = split3(jnp.sum(scaled * scaled, axis=0, keepdims=True))
    row = lax.broadcasted_iota(jnp.int32, scaled.shape, 0)
    first = 0 if left else 3
    extra = jnp.where((row >= 3 - first) & (row < 6 - first), 1.0, 0.0)
    for place, part in enumerate(norm):
        extra = jnp.where(row == first + place, part, extra)
    zero = jnp.zeros_like(extra)
    if left:
        pieces = (high, high, middle, high, middle, low, extra, zero)
    else:
        pieces = (high, middle, high, low, middle, high, extra, zero)
    return jnp.concatenate(pieces, axis=0)


def covariance(squared):
    squared = jnp.maximum(squared, TINY)
    dist = squared * lax.rsqrt(squared)
    return ((dist + LINEAR) * dist + CONSTANT) * jnp.exp2(-dist)


def product(left, right):
    return jnp.dot(left, right, preferred_element_type=f32)


def product_t(left, right):
    return lax.dot_general(left, right, (((1,), (1,)), ((), ())), preferred_element_type=f32)


def applied(dot, sides, high, low):
    rows = sides.shape[0] // 2
    both = dot(sides, high)
    return both[:rows] + both[rows:] + dot(sides[:rows], low)


def prepare_body(coords_ref, inv_ref, dir_ref, packed_ref, left_ref, sides_ref):
    scaled = coords_ref[...] * (inv_ref[...] * COORD_SCALE)
    weighted = dir_ref[...] * SCALE
    packed_ref[0:8, :] = scaled
    packed_ref[8:24, :] = weighted
    left_ref[...] = features(scaled, True).T.astype(bf16)
    sides_ref[...] = stacked(weighted)


def pair_body(left_ref, sides_ref, far_ref, near_ref, back_ref):
    sites = far_ref.shape[1]
    right = features(far_ref[0:8, :], False).astype(bf16)
    far_sides = stacked(far_ref[8:24, :])
    near = None
    for start in range(0, sites, TILE):
        columns = slice(start, start + TILE)
        values = covariance(product(left_ref[...], right[:, columns]))
        high, low = split2(values)
        part = applied(product_t, far_sides[:, columns], high, low)
        near = part if near is None else near + part
        back_ref[:, columns] = applied(product, sides_ref[...], high, low)
    near_ref[...] = near


def self_body(left_ref, sides_ref, own_ref, out_ref):
    sites = own_ref.shape[1]
    right = features(own_ref[0:8, :], False).astype(bf16)
    out_ref[...] = jnp.zeros_like(out_ref)
    for start in range(0, sites, TILE):
        stop = start + TILE
        columns = slice(start, stop)
        values = covariance(product(left_ref[0:stop, :], right[:, columns]))
        high, low = split2(values)
        out_ref[:, 0:stop] += applied(product_t, sides_ref[:, columns], high, low)
        if start:
            out_ref[:, columns] += applied(product, sides_ref[:, 0:start], high[0:start], low[0:start])


def call(body, name, shapes, cost):
    return pl.pallas_call(
        body,
        out_shape=shapes,
        compiler_params=pltpu.CompilerParams(vmem_limit_bytes=VMEM_LIMIT),
        cost_estimate=pl.CostEstimate(flops=cost, bytes_accessed=600000, transcendentals=0),
        name=name,
    )


def shape(rows, columns, dtype=f32):
    return jax.ShapeDtypeStruct((rows, columns), dtype)


def prepare(coords, inv_scale, direction):
    sites, rhs = coords.shape[1], direction.shape[0]
    shapes = (shape(8 + rhs, sites), shape(sites, 64, bf16), shape(2 * rhs, sites, bf16))
    return call(prepare_body, "prepare", shapes, 10**7)(coords, inv_scale[:, None], direction)


def pair(left, sides, far):
    out = shape(16, far.shape[1])
    return call(pair_body, "pair", (out, out), 6 * 10**9)(left, sides, far)


def own_block(left, sides, packed):
    return call(self_body, "own", shape(16, packed.shape[1]), 4 * 10**9)(left, sides, packed)


def shifted(value, steps):
    count = lax.axis_size(AXES)
    pairs = [(source, (source + steps) % count) for source in range(count)]
    return lax.ppermute(value, AXES, pairs)


def total(values):
    for axis in ("lo", "hi"):
        count = lax.axis_size(axis)
        copies = jnp.broadcast_to(values[None], (count,) + values.shape)
        values = jnp.sum(lax.all_to_all(copies, axis, 0, 0, tiled=True), axis=0)
    return values


def local(coords, inv_scale, noise_var, solution, residual, direction):
    rhs = direction.shape[0]
    packed, left, sides = prepare(coords, inv_scale, direction)
    gp_image = noise_var[None, :] * direction
    fars = [shifted(packed, offset) for offset in range(1, ROUNDS + 1)]
    returns = []
    for offset, far in zip(range(1, ROUNDS + 1), fars):
        near, back = pair(left, sides, far)
        gp_image = gp_image + near
        returns.append(shifted(back, -offset))
    own = own_block(left, sides, packed)
    gp_image = gp_image + (2.0 * ROUNDS) * own
    for back in returns:
        gp_image = gp_image + back
    sums = [
        jnp.sum(residual * residual, axis=1),
        jnp.sum(direction * gp_image, axis=1),
        jnp.sum(residual * gp_image, axis=1),
        jnp.sum(gp_image * gp_image, axis=1),
    ]
    sums = total(jnp.concatenate(sums)).reshape(4, rhs)
    old_norm, curvature, mixed, image_norm = sums[0], sums[1], sums[2], sums[3]
    step_size = old_norm / curvature
    new_norm = jnp.maximum(old_norm + step_size * (step_size * image_norm - 2.0 * mixed), 0.0)
    new_solution = solution + step_size[:, None] * direction
    new_residual = residual - step_size[:, None] * gp_image
    new_direction = new_residual + (new_norm / old_norm)[:, None] * direction
    return (new_solution, new_residual, new_direction)


def solution(mesh):
    devices = mesh.devices.reshape(-1)
    low = 32
    split = Mesh(devices.reshape(devices.size // low, low), AXES)
    columns = P(None, AXES)
    return jax.shard_map(
        local,
        mesh=split,
        in_specs=(columns, P(), P(AXES), columns, columns, columns),
        out_specs=(columns, columns, columns),
        check_vma=False,
    )
```

time: 454 us -> 96.6 us (0.21)
  blocking collectives: 239 us -> 30.9 us
  matrix products: 123 us -> 0 us
  other arithmetic: 39.3 us -> 1.22 us
  Pallas kernels: 0 us -> 21.3 us
  starting transfers between devices: 43.9 us -> 23.3 us
  waiting for transfers between devices: 3.19 us -> 16.2 us
    psum x2 -> x0, blocking collectives: 239 us -> none  [the longest x1 122 us: local(): old_norm = lax.psum(jnp.sum(residual * residual, axis=1), 'sites')]
    dot_general x66 -> x0, matrix products: 123 us -> none  [the longest x24 74.1 us: kernel_tile(): jnp.dot(left_scaled.T, right_scaled, precision=lax.Precision.HIGHEST)]
    reduce_sum x51 -> x3, other arithmetic: 38.5 us -> 0.25 us  [the longest x1 0.21 us: local(): jnp.sum(residual * residual, axis=1)]
    all_to_all x0 -> x2, blocking collectives: none -> 30.9 us  [total(): values = jnp.sum(lax.all_to_all(copies, axis, 0, 0, tiled=True), axis=0)]
    pallas_call x0 -> x5, Pallas kernels: none -> 21.3 us  [the longest x3 17.4 us: pair(): return call(pair_body, 'pair', (out, out), 6 * 10 ** 9)(left, sides, far)]
    ppermute x9 -> x6, starting transfers between devices: 43.9 us -> 23.3 us  [shifted(): return lax.ppermute(value, AXES, pairs)]
    ppermute x9 -> x6, waiting for transfers between devices: 3.19 us -> 16.2 us  [shifted(): return lax.ppermute(value, AXES, pairs)]
  transfers between devices with their start and end apart: 9 -> 6, of which waited for: 1 -> 1; matrix products, arithmetic and copies ran while one was open for 36% -> 0% of each run, Pallas kernels for 0% -> 22%
where the time goes in v1:
time: 96.6 us; the launch traced here: 96.2 us
  blocking collectives  30.9 us (32%)
  starting transfers between devices  23.3 us (24%)
  Pallas kernels  21.3 us (22%)
  waiting for transfers between devices  16.2 us (17%)
  local copies, waits for them, and re-layouts  2.46 us (3%)
  other arithmetic  1.22 us (1%)
    all_to_all x2, blocking collectives, total(): values = jnp.sum(lax.all_to_all(copies, axis, 0, 0, tiled=True), axis=0)  30.9 us
    ppermute x6, starting transfers between devices, shifted(): return lax.ppermute(value, AXES, pairs)  23.3 us
    pallas_call x3, Pallas kernels, pair(): return call(pair_body, 'pair', (out, out), 6 * 10 ** 9)(left, sides, far)  17.4 us
    ppermute x6, waiting for transfers between devices, shifted(): return lax.ppermute(value, AXES, pairs)  16.2 us
    pallas_call x1, Pallas kernels, own_block(): call(self_body, 'own', shape(16, packed.shape[1]), 4 * 10 ** 9)  3.66 us
    unnamed x14, local copies, waits for them, and re-layouts  2.36 us
  transfers between devices with their start and end apart: 6, of which 1 were waited for; matrix products, arithmetic and copies ran while one was open for 0% of the time, Pallas kernels for 22%

profile of v1, /device:TPU:1, one launch (start us, length us, event | category | flops | bytes accessed | tf_op | source)
XLA Modules:
  0.0 96.2 jit_solution(6840710420757946679)
XLA Ops:
  0.6 0.0 copy-start.6
  0.6 0.6 copy-done.6
  1.3 0.1 copy.11.inv_ref
  1.4 0.9 copy-done
  2.3 0.8 copy-done.2
  3.1 0.2 prepare.1
  3.3 7.2 %collective-permute-start.2 = (f32[24,1536]{1,0:T(8,128)S(1)}, f32[24,1536]{1,0:T(8,128)S(1)}, u32[]{:S(2)}, u32[]{:S(2)}) collective-permute-start(f32[24,1536]{1,0:T(8,128)S(1)} %get-tuple-element.14.own_ref), channel_id=1, source_target_pairs={{0,3},{1,4},{2,5},{3,6},{4,7},{5,8},{6,9},{7,10},{8,11},{9,12},{10... | collective-permute-start | bytes 442376 | tf_op jit(solution)/shard_map/ppermute | solution.py:150
  10.5 4.0 %collective-permute-start.1 = (f32[24,1536]{1,0:T(8,128)S(1)}, f32[24,1536]{1,0:T(8,128)S(1)}, u32[]{:S(2)}, u32[]{:S(2)}) collective-permute-start(f32[24,1536]{1,0:T(8,128)S(1)} %get-tuple-element.14.own_ref), channel_id=1, source_target_pairs={{0,2},{1,3},{2,4},{3,5},{4,6},{5,7},{6,8},{7,9},{8,10},{9,11},{10,... | collective-permute-start | bytes 442376 | tf_op jit(solution)/shard_map/ppermute | solution.py:150
  14.5 2.2 %collective-permute-start = (f32[24,1536]{1,0:T(8,128)S(1)}, f32[24,1536]{1,0:T(8,128)S(1)}, u32[]{:S(2)}, u32[]{:S(2)}) collective-permute-start(f32[24,1536]{1,0:T(8,128)S(1)} %get-tuple-element.14.own_ref), channel_id=1, source_target_pairs={{0,1},{1,2},{2,3},{3,4},{4,5},{5,6},{6,7},{7,8},{8,9},{9,10},{10,1... | collective-permute-start | bytes 442376 | tf_op jit(solution)/shard_map/ppermute | solution.py:150
  16.7 16.2 %collective-permute-done.2.far_ref = f32[24,1536]{1,0:T(8,128)S(1)} collective-permute-done((f32[24,1536]{1,0:T(8,128)S(1)}, f32[24,1536]{1,0:T(8,128)S(1)}, u32[]{:S(2)}, u32[]{:S(2)}) %collective-permute-start.2) | collective-permute-done | bytes 147488 | tf_op jit(solution)/shard_map/ppermute | solution.py:150
  32.9 5.8 %pair.5 = (f32[16,1536]{1,0:T(8,128)S(1)}, f32[16,1536]{1,0:T(8,128)S(1)}) custom-call(bf16[1536,64]{1,0:T(8,128)(2,1)S(1)} %get-tuple-element.12.left_ref, bf16[32,1536]{1,0:T(8,128)(2,1)S(1)} %get-tuple-element.13.sides_ref, f32[24,1536]{1,0:T(8,128)S(1)} %collective-permute-done.2.far_ref), custom_call_target="tpu_custom_call" | custom-call | flops 6000000000 | bytes 600000 | tf_op jit(solution)/shard_map/pair/pallas_call | solution.py:140
  38.7 5.3 %collective-permute-start.5 = (f32[16,1536]{1,0:T(8,128)S(1)}, f32[16,1536]{1,0:T(8,128)S(1)}, u32[]{:S(2)}, u32[]{:S(2)}) collective-permute-start(f32[16,1536]{1,0:T(8,128)S(1)} %get-tuple-element.20), channel_id=1, source_target_pairs={{0,1021},{1,1022},{2,1023},{3,0},{4,1},{5,2},{6,3},{7,4},{8,5},{9,... | collective-permute-start | bytes 294920 | tf_op jit(solution)/shard_map/ppermute | solution.py:150
  44.1 0.0 collective-permute-done.1.far_ref
  44.1 5.8 %pair.4 = (f32[16,1536]{1,0:T(8,128)S(1)}, f32[16,1536]{1,0:T(8,128)S(1)}) custom-call(bf16[1536,64]{1,0:T(8,128)(2,1)S(1)} %get-tuple-element.12.left_ref, bf16[32,1536]{1,0:T(8,128)(2,1)S(1)} %get-tuple-element.13.sides_ref, f32[24,1536]{1,0:T(8,128)S(1)} %collective-permute-done.1.far_ref), custom_call_target="tpu_custom_call" | custom-call | flops 6000000000 | bytes 600000 | tf_op jit(solution)/shard_map/pair/pallas_call | solution.py:140
  49.9 2.1 %collective-permute-start.4 = (f32[16,1536]{1,0:T(8,128)S(1)}, f32[16,1536]{1,0:T(8,128)S(1)}, u32[]{:S(2)}, u32[]{:S(2)}) collective-permute-start(f32[16,1536]{1,0:T(8,128)S(1)} %get-tuple-element.19), channel_id=1, source_target_pairs={{0,1022},{1,1023},{2,0},{3,1},{4,2},{5,3},{6,4},{7,5},{8,6},{9,7},... | collective-permute-start | bytes 294920 | tf_op jit(solution)/shard_map/ppermute | solution.py:150
  52.0 0.0 collective-permute-done.far_ref
  52.0 5.8 %pair.3 = (f32[16,1536]{1,0:T(8,128)S(1)}, f32[16,1536]{1,0:T(8,128)S(1)}) custom-call(bf16[1536,64]{1,0:T(8,128)(2,1)S(1)} %get-tuple-element.12.left_ref, bf16[32,1536]{1,0:T(8,128)(2,1)S(1)} %get-tuple-element.13.sides_ref, f32[24,1536]{1,0:T(8,128)S(1)} %collective-permute-done.far_ref), custom_call_target="tpu_custom_call" | custom-call | flops 6000000000 | bytes 600000 | tf_op jit(solution)/shard_map/pair/pallas_call | solution.py:140
  57.8 2.5 %collective-permute-start.3 = (f32[16,1536]{1,0:T(8,128)S(1)}, f32[16,1536]{1,0:T(8,128)S(1)}, u32[]{:S(2)}, u32[]{:S(2)}) collective-permute-start(f32[16,1536]{1,0:T(8,128)S(1)} %get-tuple-element.18), channel_id=1, source_target_pairs={{0,1023},{1,0},{2,1},{3,2},{4,3},{5,4},{6,5},{7,6},{8,7},{9,8},{10... | collective-permute-start | bytes 294920 | tf_op jit(solution)/shard_map/ppermute | solution.py:150
  60.3 0.0 copy-start.5
  60.3 3.7 %own.1 = f32[16,1536]{1,0:T(8,128)S(1)} custom-call(bf16[1536,64]{1,0:T(8,128)(2,1)S(1)} %get-tuple-element.12.left_ref, bf16[32,1536]{1,0:T(8,128)(2,1)S(1)} %get-tuple-element.13.sides_ref, f32[24,1536]{1,0:T(8,128)S(1)} %get-tuple-element.14.own_ref), custom_call_target="tpu_custom_call" | custom-call | flops 4000000000 | bytes 600000 | tf_op jit(solution)/shard_map/own/pallas_call | solution.py:144
  64.0 0.0 collective-permute-done.5
  64.0 0.0 collective-permute-done.4
  64.0 0.0 collective-permute-done.3
  64.0 0.0 copy-done.1
  64.0 0.0 copy-done.3
  64.0 0.2 multiply_reduce_fusion.3
  64.2 0.1 pad_maximum_fusion
  64.3 16.2 %all_to_all.12 = f32[32,1,64]{2,1,0:T(1,128)S(1)} all-to-all(f32[32,1,64]{2,1,0:T(1,128)S(1)} %broadcast_in_dim.7), channel_id=1, replica_groups=mesh['hi'=32,'lo'=32] {'lo'}, dimensions={0} | all-to-all | bytes 16384 | tf_op jit(solution)/shard_map/all_to_all | solution.py:157
  80.6 14.6 %all_to_all.13 = f32[32,1,64]{2,1,0:T(1,128)S(1)} all-to-all(f32[32,1,64]{2,1,0:T(1,128)S(1)} %broadcast_in_dim.8), channel_id=1, replica_groups=mesh['hi'=32,'lo'=32] {'hi'}, dimensions={0} | all-to-all | bytes 16384 | tf_op jit(solution)/shard_map/all_to_all | solution.py:157
  95.3 0.1 maximum_divide_fusion
  95.4 0.0 copy-done.4
  95.4 0.8 multiply_add_fusion
  (10 shorter events, 0.1 us)
Async XLA Ops:
  0.6 0.7 copy-start.6
  1.4 0.9 copy-start
  2.3 0.8 copy-start.2
  3.3 29.6 %collective-permute-start.2 = (f32[24,1536]{1,0:T(8,128)S(1)}, f32[24,1536]{1,0:T(8,128)S(1)}, u32[]{:S(2)}, u32[]{:S(2)}) collective-permute-start(f32[24,1536]{1,0:T(8,128)S(1)} %get-tuple-element.14.own_ref), channel_id=1, source_target_pairs={{0,3},{1,4},{2,5},{3,6},{4,7},{5,8},{6,9},{7,10},{8,11},{9,12},{10... | collective-permute-start | bytes 442376 | tf_op jit(solution)/shard_map/ppermute | solution.py:150
  10.5 33.6 %collective-permute-start.1 = (f32[24,1536]{1,0:T(8,128)S(1)}, f32[24,1536]{1,0:T(8,128)S(1)}, u32[]{:S(2)}, u32[]{:S(2)}) collective-permute-start(f32[24,1536]{1,0:T(8,128)S(1)} %get-tuple-element.14.own_ref), channel_id=1, source_target_pairs={{0,2},{1,3},{2,4},{3,5},{4,6},{5,7},{6,8},{7,9},{8,10},{9,11},{10,... | collective-permute-start | bytes 442376 | tf_op jit(solution)/shard_map/ppermute | solution.py:150
  14.5 37.5 %collective-permute-start = (f32[24,1536]{1,0:T(8,128)S(1)}, f32[24,1536]{1,0:T(8,128)S(1)}, u32[]{:S(2)}, u32[]{:S(2)}) collective-permute-start(f32[24,1536]{1,0:T(8,128)S(1)} %get-tuple-element.14.own_ref), channel_id=1, source_target_pairs={{0,1},{1,2},{2,3},{3,4},{4,5},{5,6},{6,7},{7,8},{8,9},{9,10},{10,1... | collective-permute-start | bytes 442376 | tf_op jit(solution)/shard_map/ppermute | solution.py:150
  38.7 25.2 %collective-permute-start.5 = (f32[16,1536]{1,0:T(8,128)S(1)}, f32[16,1536]{1,0:T(8,128)S(1)}, u32[]{:S(2)}, u32[]{:S(2)}) collective-permute-start(f32[16,1536]{1,0:T(8,128)S(1)} %get-tuple-element.20), channel_id=1, source_target_pairs={{0,1021},{1,1022},{2,1023},{3,0},{4,1},{5,2},{6,3},{7,4},{8,5},{9,... | collective-permute-start | bytes 294920 | tf_op jit(solution)/shard_map/ppermute | solution.py:150
  49.9 14.1 %collective-permute-start.4 = (f32[16,1536]{1,0:T(8,128)S(1)}, f32[16,1536]{1,0:T(8,128)S(1)}, u32[]{:S(2)}, u32[]{:S(2)}) collective-permute-start(f32[16,1536]{1,0:T(8,128)S(1)} %get-tuple-element.19), channel_id=1, source_target_pairs={{0,1022},{1,1023},{2,0},{3,1},{4,2},{5,3},{6,4},{7,5},{8,6},{9,7},... | collective-permute-start | bytes 294920 | tf_op jit(solution)/shard_map/ppermute | solution.py:150
  57.8 6.2 %copy-start.1 = (f32[16,1536]{1,0:T(8,128)S(1)}, f32[16,1536]{1,0:T(8,128)}, u32[]{:S(2)}) copy-start(f32[16,1536]{1,0:T(8,128)} %dir_ref.1) | copy-start | bytes 294916
  57.8 6.2 %copy-start.3 = (f32[16,1536]{1,0:T(8,128)S(1)}, f32[16,1536]{1,0:T(8,128)}, u32[]{:S(2)}) copy-start(f32[16,1536]{1,0:T(8,128)} %param.10) | copy-start | bytes 294916
  57.8 6.2 %collective-permute-start.3 = (f32[16,1536]{1,0:T(8,128)S(1)}, f32[16,1536]{1,0:T(8,128)S(1)}, u32[]{:S(2)}, u32[]{:S(2)}) collective-permute-start(f32[16,1536]{1,0:T(8,128)S(1)} %get-tuple-element.18), channel_id=1, source_target_pairs={{0,1023},{1,0},{2,1},{3,2},{4,3},{5,4},{6,5},{7,6},{8,7},{9,8},{10... | collective-permute-start | bytes 294920 | tf_op jit(solution)/shard_map/ppermute | solution.py:150
  60.3 3.7 %copy-start.5 = (f32[1536]{0:T(1024)S(1)}, f32[1536]{0:T(1024)}, u32[]{:S(2)}) copy-start(f32[1536]{0:T(1024)} %param.8) | copy-start | bytes 18436
  64.2 31.1 %copy-start.4 = (f32[16,1536]{1,0:T(8,128)S(1)}, f32[16,1536]{1,0:T(8,128)}, u32[]{:S(2)}) copy-start(f32[16,1536]{1,0:T(8,128)} %param.9) | copy-start | bytes 294916

commit v2 on v1

--- a/solution.py
+++ b/solution.py
@@ -77,27 +77,26 @@
     return both[:rows] + both[rows:] + dot(sides[:rows], low)
 
 
-def prepare_body(coords_ref, inv_ref, dir_ref, packed_ref, left_ref, sides_ref):
-    scaled = coords_ref[...] * (inv_ref[...] * COORD_SCALE)
-    weighted = dir_ref[...] * SCALE
-    packed_ref[0:8, :] = scaled
-    packed_ref[8:24, :] = weighted
-    left_ref[...] = features(scaled, True).T.astype(bf16)
-    sides_ref[...] = stacked(weighted)
-
-
-def pair_body(left_ref, sides_ref, far_ref, near_ref, back_ref):
-    sites = far_ref.shape[1]
-    right = features(far_ref[0:8, :], False).astype(bf16)
-    far_sides = stacked(far_ref[8:24, :])
+def prepare_body(packed_ref, left_ref, sides_ref):
+    left_ref[...] = features(packed_ref[0:8, :], True).T.astype(bf16)
+    sides_ref[...] = stacked(packed_ref[8:24, :])
+
+
+def pairs_body(count, left_ref, sides_ref, *refs):
+    fars, near_ref, back_ref = refs[:count], refs[count], refs[count + 1]
     near = None
-    for start in range(0, sites, TILE):
-        columns = slice(start, start + TILE)
-        values = covariance(product(left_ref[...], right[:, columns]))
-        high, low = split2(values)
-        part = applied(product_t, far_sides[:, columns], high, low)
-        near = part if near is None else near + part
-        back_ref[:, columns] = applied(product, sides_ref[...], high, low)
+    for place, far_ref in enumerate(fars):
+        sites = far_ref.shape[1]
+        rows = slice(16 * place, 16 * place + 16)
+        right = features(far_ref[0:8, :], False).astype(bf16)
+        far_sides = stacked(far_ref[8:24, :])
+        for start in range(0, sites, TILE):
+            columns = slice(start, start + TILE)
+            values = covariance(product(left_ref[...], right[:, columns]))
+            high, low = split2(values)
+            part = applied(product_t, far_sides[:, columns], high, low)
+            near = part if near is None else near + part
+            back_ref[rows, columns] = applied(product, sides_ref[...], high, low)
     near_ref[...] = near
 
 
@@ -129,15 +128,17 @@
     return jax.ShapeDtypeStruct((rows, columns), dtype)
 
 
-def prepare(coords, inv_scale, direction):
-    sites, rhs = coords.shape[1], direction.shape[0]
-    shapes = (shape(8 + rhs, sites), shape(sites, 64, bf16), shape(2 * rhs, sites, bf16))
-    return call(prepare_body, "prepare", shapes, 10**7)(coords, inv_scale[:, None], direction)
-
-
-def pair(left, sides, far):
-    out = shape(16, far.shape[1])
-    return call(pair_body, "pair", (out, out), 6 * 10**9)(left, sides, far)
+def prepare(packed):
+    rows, sites = packed.shape
+    shapes = (shape(sites, 64, bf16), shape(2 * (rows - 8), sites, bf16))
+    return call(prepare_body, "prepare", shapes, 10**7)(packed)
+
+
+def pairs(left, sides, fars):
+    count, sites = len(fars), fars[0].shape[1]
+    body = functools.partial(pairs_body, count)
+    shapes = (shape(16, sites), shape(16 * count, sites))
+    return call(body, "pairs%d" % count, shapes, 6 * count * 10**9)(left, sides, *fars)
 
 
 def own_block(left, sides, packed):
@@ -160,18 +161,19 @@
 
 def local(coords, inv_scale, noise_var, solution, residual, direction):
     rhs = direction.shape[0]
-    packed, left, sides = prepare(coords, inv_scale, direction)
+    scaled = coords * (inv_scale * COORD_SCALE)[:, None]
+    packed = jnp.concatenate([scaled, direction * SCALE], axis=0)
+    left, sides = prepare(packed)
     gp_image = noise_var[None, :] * direction
-    fars = [shifted(packed, offset) for offset in range(1, ROUNDS + 1)]
-    returns = []
-    for offset, far in zip(range(1, ROUNDS + 1), fars):
-        near, back = pair(left, sides, far)
-        gp_image = gp_image + near
-        returns.append(shifted(back, -offset))
+    second = shifted(packed, 2)
+    third = shifted(packed, 3)
+    first = shifted(packed, 1)
+    near, back = pairs(left, sides, [second, third])
+    arrived = shifted(back, -2)
+    near_first, back_first = pairs(left, sides, [first])
+    returned = shifted(back_first + arrived[rhs:], -1)
     own = own_block(left, sides, packed)
-    gp_image = gp_image + (2.0 * ROUNDS) * own
-    for back in returns:
-        gp_image = gp_image + back
+    gp_image = gp_image + near + near_first + (2.0 * ROUNDS) * own + arrived[:rhs] + returned
     sums = [
         jnp.sum(residual * residual, axis=1),
         jnp.sum(direction * gp_image, axis=1),

time: 96.6 us -> 100 us (1.035)
  waiting for transfers between devices: 16.2 us -> 20.6 us
  blocking collectives: 30.9 us -> 34.9 us
  starting transfers between devices: 23.3 us -> 19.3 us
  local copies, waits for them, and re-layouts: 2.46 us -> 0.06 us
  other arithmetic: 1.22 us -> 2.24 us
    ppermute x6 -> x5, waiting for transfers between devices: 16.2 us -> 20.6 us  [shifted(): return lax.ppermute(value, AXES, pairs)]
    all_to_all x2, blocking collectives: 30.9 us -> 34.9 us  [total(): values = jnp.sum(lax.all_to_all(copies, axis, 0, 0, tiled=True), axis=0)]
    ppermute x6 -> x5, starting transfers between devices: 23.3 us -> 19.3 us  [shifted(): return lax.ppermute(value, AXES, pairs)]
    unnamed x14 -> x12, local copies, waits for them, and re-layouts: 2.36 us -> 0.03 us
    mul x0 -> x3, other arithmetic: none -> 1 us  [the longest x1 0.92 us: local(): packed = jnp.concatenate([scaled, direction * SCALE], axis=0)]
    pallas_call x4 -> x3, Pallas kernels: 17.7 us -> 18 us  [the longest x2 17.9 us: pairs(): call(body, 'pairs%d' % count, shapes, 6 * count * 10 ** 9)]
  transfers between devices with their start and end apart: 6 -> 5, of which waited for: 1 -> 3; matrix products, arithmetic and copies ran while one was open for 0% -> 0% of each run, Pallas kernels for 22% -> 22%
where the time goes in v2:
time: 100 us; the launch traced here: 99.6 us
  blocking collectives  34.9 us (35%)
  Pallas kernels  21.7 us (22%)
  waiting for transfers between devices  20.6 us (21%)
  starting transfers between devices  19.3 us (19%)
  other arithmetic  2.24 us (2%)
    all_to_all x2, blocking collectives, total(): values = jnp.sum(lax.all_to_all(copies, axis, 0, 0, tiled=True), axis=0)  34.9 us
    ppermute x5, waiting for transfers between devices, shifted(): return lax.ppermute(value, AXES, pairs)  20.6 us
    ppermute x5, starting transfers between devices, shifted(): return lax.ppermute(value, AXES, pairs)  19.3 us
    pallas_call x2, Pallas kernels, pairs(): call(body, 'pairs%d' % count, shapes, 6 * count * 10 ** 9)  17.9 us
    pallas_call x1, Pallas kernels, own_block(): call(self_body, 'own', shape(16, packed.shape[1]), 4 * 10 ** 9)  3.66 us
  transfers between devices with their start and end apart: 5, of which 3 were waited for; matrix products, arithmetic and copies ran while one was open for 0% of the time, Pallas kernels for 22%

profile of v2, /device:TPU:1, one launch (start us, length us, event | category | flops | bytes accessed | tf_op | source)
XLA Modules:
  0.0 99.6 jit_solution(14891484712568727896)
XLA Ops:
  0.6 0.0 copy-start.5
  0.6 0.0 copy-start.3
  0.6 0.9 broadcast_multiply_fusion
  1.6 0.0 copy-done.5
  1.6 0.0 copy-done.3
  1.6 0.1 broadcast_multiply_fusion.1
  1.7 4.8 %collective-permute-start = (f32[24,1536]{1,0:T(8,128)S(1)}, f32[24,1536]{1,0:T(8,128)S(1)}, u32[]{:S(2)}, u32[]{:S(2)}) collective-permute-start(f32[24,1536]{1,0:T(8,128)S(1)} %pad_maximum_fusion.packed_ref.own_ref), channel_id=1, source_target_pairs={{0,2},{1,3},{2,4},{3,5},{4,6},{5,7},{6,8},{7,9},{8,10},{9,11},{10,... | collective-permute-start | bytes 442376 | tf_op jit(solution)/shard_map/ppermute | solution.py:151
  6.5 6.6 %collective-permute-start.1 = (f32[24,1536]{1,0:T(8,128)S(1)}, f32[24,1536]{1,0:T(8,128)S(1)}, u32[]{:S(2)}, u32[]{:S(2)}) collective-permute-start(f32[24,1536]{1,0:T(8,128)S(1)} %pad_maximum_fusion.packed_ref.own_ref), channel_id=1, source_target_pairs={{0,3},{1,4},{2,5},{3,6},{4,7},{5,8},{6,9},{7,10},{8,11},{9,12},{10... | collective-permute-start | bytes 442376 | tf_op jit(solution)/shard_map/ppermute | solution.py:151
  13.2 1.9 %collective-permute-start.2 = (f32[24,1536]{1,0:T(8,128)S(1)}, f32[24,1536]{1,0:T(8,128)S(1)}, u32[]{:S(2)}, u32[]{:S(2)}) collective-permute-start(f32[24,1536]{1,0:T(8,128)S(1)} %pad_maximum_fusion.packed_ref.own_ref), channel_id=1, source_target_pairs={{0,1},{1,2},{2,3},{3,4},{4,5},{5,6},{6,7},{7,8},{8,9},{9,10},{10,1... | collective-permute-start | bytes 442376 | tf_op jit(solution)/shard_map/ppermute | solution.py:151
  15.1 0.2 prepare.1
  15.3 13.8 %collective-permute-done.refs_0_ = f32[24,1536]{1,0:T(8,128)S(1)} collective-permute-done((f32[24,1536]{1,0:T(8,128)S(1)}, f32[24,1536]{1,0:T(8,128)S(1)}, u32[]{:S(2)}, u32[]{:S(2)}) %collective-permute-start) | collective-permute-done | bytes 147488 | tf_op jit(solution)/shard_map/ppermute | solution.py:151
  29.1 6.4 %collective-permute-done.1.refs_1_ = f32[24,1536]{1,0:T(8,128)S(1)} collective-permute-done((f32[24,1536]{1,0:T(8,128)S(1)}, f32[24,1536]{1,0:T(8,128)S(1)}, u32[]{:S(2)}, u32[]{:S(2)}) %collective-permute-start.1) | collective-permute-done | bytes 147488 | tf_op jit(solution)/shard_map/ppermute | solution.py:151
  35.5 12.1 %pairs2.1 = (f32[16,1536]{1,0:T(8,128)S(1)}, f32[32,1536]{1,0:T(8,128)S(1)}) custom-call(bf16[1536,64]{1,0:T(8,128)(2,1)S(1)} %get-tuple-element.9.left_ref, bf16[32,1536]{1,0:T(8,128)(2,1)S(1)} %get-tuple-element.10.sides_ref, f32[24,1536]{1,0:T(8,128)S(1)} %collective-permute-done.refs_0_, f32[24,1536]{1,0:T(8,128)S(1)} %collective-permute-done.1.refs_1_), custom_call_target="tpu_custom_call" | custom-call | flops 12000000000 | bytes 600000 | tf_op jit(solution)/shard_map/pairs2/pallas_call | solution.py:141
  47.6 3.9 %collective-permute-start.3 = (f32[32,1536]{1,0:T(8,128)S(1)}, f32[32,1536]{1,0:T(8,128)S(1)}, u32[]{:S(2)}, u32[]{:S(2)}) collective-permute-start(f32[32,1536]{1,0:T(8,128)S(1)} %get-tuple-element.13), channel_id=1, source_target_pairs={{0,1022},{1,1023},{2,0},{3,1},{4,2},{5,3},{6,4},{7,5},{8,6},{9,7},... | collective-permute-start | bytes 589832 | tf_op jit(solution)/shard_map/ppermute | solution.py:151
  51.5 0.0 collective-permute-done.2.refs_0_
  51.5 5.8 %pairs1.1 = (f32[16,1536]{1,0:T(8,128)S(1)}, f32[16,1536]{1,0:T(8,128)S(1)}) custom-call(bf16[1536,64]{1,0:T(8,128)(2,1)S(1)} %get-tuple-element.9.left_ref, bf16[32,1536]{1,0:T(8,128)(2,1)S(1)} %get-tuple-element.10.sides_ref, f32[24,1536]{1,0:T(8,128)S(1)} %collective-permute-done.2.refs_0_), custom_call_target="tpu_custom_call" | custom-call | flops 6000000000 | bytes 600000 | tf_op jit(solution)/shard_map/pairs1/pallas_call | solution.py:141
  57.3 0.0 collective-permute-done.3
  57.3 0.0 copy-start
  57.3 0.0 copy-start.1
  57.4 2.1 %collective-permute-start.4 = (f32[16,1536]{1,0:T(8,128)S(1)}, f32[16,1536]{1,0:T(8,128)S(1)}, u32[]{:S(2)}, u32[]{:S(2)}) collective-permute-start(f32[16,1536]{1,0:T(8,128)S(1)} %slice_add_fusion), channel_id=1, source_target_pairs={{0,1023},{1,0},{2,1},{3,2},{4,3},{5,4},{6,5},{7,6},{8,7},{9,8},{10... | collective-permute-start | bytes 294920 | tf_op jit(solution)/shard_map/ppermute | solution.py:151
  59.4 0.0 copy-start.4
  59.4 3.7 %own.1 = f32[16,1536]{1,0:T(8,128)S(1)} custom-call(bf16[1536,64]{1,0:T(8,128)(2,1)S(1)} %get-tuple-element.9.left_ref, bf16[32,1536]{1,0:T(8,128)(2,1)S(1)} %get-tuple-element.10.sides_ref, f32[24,1536]{1,0:T(8,128)S(1)} %pad_maximum_fusion.packed_ref.own_ref), custom_call_target="tpu_custom_call" | custom-call | flops 4000000000 | bytes 600000 | tf_op jit(solution)/shard_map/own/pallas_call | solution.py:145
  63.1 0.3 collective-permute-done.4
  63.4 0.0 copy-done
  63.4 0.0 copy-done.1
  63.4 0.0 copy-done.4
  63.4 0.2 multiply_reduce_fusion.3
  63.6 0.1 pad_maximum_fusion.1
  63.7 20.3 %all_to_all.12 = f32[32,1,64]{2,1,0:T(1,128)S(1)} all-to-all(f32[32,1,64]{2,1,0:T(1,128)S(1)} %broadcast_in_dim.4), channel_id=1, replica_groups=mesh['hi'=32,'lo'=32] {'lo'}, dimensions={0} | all-to-all | bytes 16384 | tf_op jit(solution)/shard_map/all_to_all | solution.py:158
  84.0 14.7 %all_to_all.13 = f32[32,1,64]{2,1,0:T(1,128)S(1)} all-to-all(f32[32,1,64]{2,1,0:T(1,128)S(1)} %broadcast_in_dim.5), channel_id=1, replica_groups=mesh['hi'=32,'lo'=32] {'hi'}, dimensions={0} | all-to-all | bytes 16384 | tf_op jit(solution)/shard_map/all_to_all | solution.py:158
  98.7 0.1 maximum_divide_fusion
  98.8 0.8 multiply_add_fusion
  (9 shorter events, 0.1 us)
Async XLA Ops:
  0.6 0.9 copy-start.5
  0.6 1.0 copy-start.3
  1.7 27.4 %collective-permute-start = (f32[24,1536]{1,0:T(8,128)S(1)}, f32[24,1536]{1,0:T(8,128)S(1)}, u32[]{:S(2)}, u32[]{:S(2)}) collective-permute-start(f32[24,1536]{1,0:T(8,128)S(1)} %pad_maximum_fusion.packed_ref.own_ref), channel_id=1, source_target_pairs={{0,2},{1,3},{2,4},{3,5},{4,6},{5,7},{6,8},{7,9},{8,10},{9,11},{10,... | collective-permute-start | bytes 442376 | tf_op jit(solution)/shard_map/ppermute | solution.py:151
  6.5 29.0 %collective-permute-start.1 = (f32[24,1536]{1,0:T(8,128)S(1)}, f32[24,1536]{1,0:T(8,128)S(1)}, u32[]{:S(2)}, u32[]{:S(2)}) collective-permute-start(f32[24,1536]{1,0:T(8,128)S(1)} %pad_maximum_fusion.packed_ref.own_ref), channel_id=1, source_target_pairs={{0,3},{1,4},{2,5},{3,6},{4,7},{5,8},{6,9},{7,10},{8,11},{9,12},{10... | collective-permute-start | bytes 442376 | tf_op jit(solution)/shard_map/ppermute | solution.py:151
  13.2 38.3 %collective-permute-start.2 = (f32[24,1536]{1,0:T(8,128)S(1)}, f32[24,1536]{1,0:T(8,128)S(1)}, u32[]{:S(2)}, u32[]{:S(2)}) collective-permute-start(f32[24,1536]{1,0:T(8,128)S(1)} %pad_maximum_fusion.packed_ref.own_ref), channel_id=1, source_target_pairs={{0,1},{1,2},{2,3},{3,4},{4,5},{5,6},{6,7},{7,8},{8,9},{9,10},{10,1... | collective-permute-start | bytes 442376 | tf_op jit(solution)/shard_map/ppermute | solution.py:151
  47.6 9.7 %collective-permute-start.3 = (f32[32,1536]{1,0:T(8,128)S(1)}, f32[32,1536]{1,0:T(8,128)S(1)}, u32[]{:S(2)}, u32[]{:S(2)}) collective-permute-start(f32[32,1536]{1,0:T(8,128)S(1)} %get-tuple-element.13), channel_id=1, source_target_pairs={{0,1022},{1,1023},{2,0},{3,1},{4,2},{5,3},{6,4},{7,5},{8,6},{9,7},... | collective-permute-start | bytes 589832 | tf_op jit(solution)/shard_map/ppermute | solution.py:151
  57.3 6.1 %copy-start = (f32[16,1536]{1,0:T(8,128)S(1)}, f32[16,1536]{1,0:T(8,128)}, u32[]{:S(2)}) copy-start(f32[16,1536]{1,0:T(8,128)} %param.11) | copy-start | bytes 294916
  57.3 6.1 %copy-start.1 = (f32[16,1536]{1,0:T(8,128)S(1)}, f32[16,1536]{1,0:T(8,128)}, u32[]{:S(2)}) copy-start(f32[16,1536]{1,0:T(8,128)} %param.10) | copy-start | bytes 294916
  57.4 6.1 %collective-permute-start.4 = (f32[16,1536]{1,0:T(8,128)S(1)}, f32[16,1536]{1,0:T(8,128)S(1)}, u32[]{:S(2)}, u32[]{:S(2)}) collective-permute-start(f32[16,1536]{1,0:T(8,128)S(1)} %slice_add_fusion), channel_id=1, source_target_pairs={{0,1023},{1,0},{2,1},{3,2},{4,3},{5,4},{6,5},{7,6},{8,7},{9,8},{10... | collective-permute-start | bytes 294920 | tf_op jit(solution)/shard_map/ppermute | solution.py:151
  59.4 4.0 %copy-start.4 = (f32[1536]{0:T(1024)S(1)}, f32[1536]{0:T(1024)}, u32[]{:S(2)}) copy-start(f32[1536]{0:T(1024)} %param.8) | copy-start | bytes 18436
  63.6 35.2 %copy-start.2 = (f32[16,1536]{1,0:T(8,128)S(1)}, f32[16,1536]{1,0:T(8,128)}, u32[]{:S(2)}) copy-start(f32[16,1536]{1,0:T(8,128)} %param.9) | copy-start | bytes 294916

commit v3 on v2

--- a/solution.py
+++ b/solution.py
@@ -165,15 +165,16 @@
     packed = jnp.concatenate([scaled, direction * SCALE], axis=0)
     left, sides = prepare(packed)
     gp_image = noise_var[None, :] * direction
-    second = shifted(packed, 2)
-    third = shifted(packed, 3)
-    first = shifted(packed, 1)
-    near, back = pairs(left, sides, [second, third])
-    arrived = shifted(back, -2)
-    near_first, back_first = pairs(left, sides, [first])
-    returned = shifted(back_first + arrived[rhs:], -1)
-    own = own_block(left, sides, packed)
-    gp_image = gp_image + near + near_first + (2.0 * ROUNDS) * own + arrived[:rhs] + returned
+    offsets = (-2, 3, 1)
+    fars = [shifted(packed, offset) for offset in offsets]
+    returns = []
+    for offset, far in zip(offsets, fars):
+        near, back = pairs(left, sides, [far])
+        gp_image = gp_image + near
+        returns.append(shifted(back, -offset))
+    gp_image = gp_image + (2.0 * ROUNDS) * own_block(left, sides, packed)
+    for back in returns:
+        gp_image = gp_image + back
     sums = [
         jnp.sum(residual * residual, axis=1),
         jnp.sum(direction * gp_image, axis=1),

time: 100 us -> 99.9 us (level)
  waiting for transfers between devices: 20.6 us -> 2.32 us
  starting transfers between devices: 19.3 us -> 36.1 us
  blocking collectives: 34.9 us -> 36.1 us
    ppermute x5 -> x6, waiting for transfers between devices: 20.6 us -> 2.32 us  [shifted(): return lax.ppermute(value, AXES, pairs)]
    ppermute x5 -> x6, starting transfers between devices: 19.3 us -> 36.1 us  [shifted(): return lax.ppermute(value, AXES, pairs)]
    all_to_all x2, blocking collectives: 34.9 us -> 36.1 us  [total(): values = jnp.sum(lax.all_to_all(copies, axis, 0, 0, tiled=True), axis=0)]
    pallas_call x2 -> x3, Pallas kernels: 17.9 us -> 17.4 us  [pairs(): call(body, 'pairs%d' % count, shapes, 6 * count * 10 ** 9)]
  transfers between devices with their start and end apart: 5 -> 6, of which waited for: 3 -> 2; matrix products, arithmetic and copies ran while one was open for 0% -> 0% of each run, Pallas kernels for 22% -> 21%
where the time goes in v3:
time: 99.9 us; the launch traced here: 99.5 us
  starting transfers between devices  36.1 us (36%)
  blocking collectives  36.1 us (36%)
  Pallas kernels  21.3 us (21%)
  other arithmetic  2.86 us (3%)
  waiting for transfers between devices  2.32 us (2%)
    all_to_all x2, blocking collectives, total(): values = jnp.sum(lax.all_to_all(copies, axis, 0, 0, tiled=True), axis=0)  36.1 us
    ppermute x6, starting transfers between devices, shifted(): return lax.ppermute(value, AXES, pairs)  36.1 us
    pallas_call x3, Pallas kernels, pairs(): call(body, 'pairs%d' % count, shapes, 6 * count * 10 ** 9)  17.4 us
    pallas_call x1, Pallas kernels, own_block(): call(self_body, 'own', shape(16, packed.shape[1]), 4 * 10 ** 9)  3.66 us
    ppermute x6, waiting for transfers between devices, shifted(): return lax.ppermute(value, AXES, pairs)  2.32 us
  transfers between devices with their start and end apart: 6, of which 2 were waited for; matrix products, arithmetic and copies ran while one was open for 0% of the time, Pallas kernels for 21%

profile of v3, /device:TPU:1, one launch (start us, length us, event | category | flops | bytes accessed | tf_op | source)
XLA Modules:
  0.0 99.5 jit_solution(2378529684824300769)
XLA Ops:
  0.6 0.7 broadcast_multiply_fusion.2
  1.3 0.9 broadcast_multiply_fusion
  2.2 0.0 copy-done.3
  2.2 0.1 broadcast_multiply_fusion.1
  2.3 7.2 %collective-permute-start.1 = (f32[24,1536]{1,0:T(8,128)S(1)}, f32[24,1536]{1,0:T(8,128)S(1)}, u32[]{:S(2)}, u32[]{:S(2)}) collective-permute-start(f32[24,1536]{1,0:T(8,128)S(1)} %pad_maximum_fusion.packed_ref.own_ref), channel_id=1, source_target_pairs={{0,3},{1,4},{2,5},{3,6},{4,7},{5,8},{6,9},{7,10},{8,11},{9,12},{10... | collective-permute-start | bytes 442376 | tf_op jit(solution)/shard_map/ppermute | solution.py:151
  9.5 1.9 %collective-permute-start.2 = (f32[24,1536]{1,0:T(8,128)S(1)}, f32[24,1536]{1,0:T(8,128)S(1)}, u32[]{:S(2)}, u32[]{:S(2)}) collective-permute-start(f32[24,1536]{1,0:T(8,128)S(1)} %pad_maximum_fusion.packed_ref.own_ref), channel_id=1, source_target_pairs={{0,1},{1,2},{2,3},{3,4},{4,5},{5,6},{6,7},{7,8},{8,9},{9,10},{10,1... | collective-permute-start | bytes 442376 | tf_op jit(solution)/shard_map/ppermute | solution.py:151
  11.4 18.6 %collective-permute-start = (f32[24,1536]{1,0:T(8,128)S(1)}, f32[24,1536]{1,0:T(8,128)S(1)}, u32[]{:S(2)}, u32[]{:S(2)}) collective-permute-start(f32[24,1536]{1,0:T(8,128)S(1)} %pad_maximum_fusion.packed_ref.own_ref), channel_id=1, source_target_pairs={{0,1022},{1,1023},{2,0},{3,1},{4,2},{5,3},{6,4},{7,5},{8,6},{9,7},... | collective-permute-start | bytes 442376 | tf_op jit(solution)/shard_map/ppermute | solution.py:151
  30.0 0.2 prepare.1
  30.2 2.0 %collective-permute-done.1.refs_0_ = f32[24,1536]{1,0:T(8,128)S(1)} collective-permute-done((f32[24,1536]{1,0:T(8,128)S(1)}, f32[24,1536]{1,0:T(8,128)S(1)}, u32[]{:S(2)}, u32[]{:S(2)}) %collective-permute-start.1) | collective-permute-done | bytes 147488 | tf_op jit(solution)/shard_map/ppermute | solution.py:151
  32.2 5.8 %pairs1.4 = (f32[16,1536]{1,0:T(8,128)S(1)}, f32[16,1536]{1,0:T(8,128)S(1)}) custom-call(bf16[1536,64]{1,0:T(8,128)(2,1)S(1)} %get-tuple-element.11.left_ref, bf16[32,1536]{1,0:T(8,128)(2,1)S(1)} %get-tuple-element.12.sides_ref, f32[24,1536]{1,0:T(8,128)S(1)} %collective-permute-done.1.refs_0_), custom_call_target="tpu_custom_call" | custom-call | flops 6000000000 | bytes 600000 | tf_op jit(solution)/shard_map/pairs1/pallas_call | solution.py:141
  38.0 4.2 %collective-permute-start.4 = (f32[16,1536]{1,0:T(8,128)S(1)}, f32[16,1536]{1,0:T(8,128)S(1)}, u32[]{:S(2)}, u32[]{:S(2)}) collective-permute-start(f32[16,1536]{1,0:T(8,128)S(1)} %get-tuple-element.17), channel_id=1, source_target_pairs={{0,1021},{1,1022},{2,1023},{3,0},{4,1},{5,2},{6,3},{7,4},{8,5},{9,... | collective-permute-start | bytes 294920 | tf_op jit(solution)/shard_map/ppermute | solution.py:151
  42.2 0.0 collective-permute-done.refs_0_
  42.3 5.8 %pairs1.3 = (f32[16,1536]{1,0:T(8,128)S(1)}, f32[16,1536]{1,0:T(8,128)S(1)}) custom-call(bf16[1536,64]{1,0:T(8,128)(2,1)S(1)} %get-tuple-element.11.left_ref, bf16[32,1536]{1,0:T(8,128)(2,1)S(1)} %get-tuple-element.12.sides_ref, f32[24,1536]{1,0:T(8,128)S(1)} %collective-permute-done.refs_0_), custom_call_target="tpu_custom_call" | custom-call | flops 6000000000 | bytes 600000 | tf_op jit(solution)/shard_map/pairs1/pallas_call | solution.py:141
  48.1 2.1 %collective-permute-start.3 = (f32[16,1536]{1,0:T(8,128)S(1)}, f32[16,1536]{1,0:T(8,128)S(1)}, u32[]{:S(2)}, u32[]{:S(2)}) collective-permute-start(f32[16,1536]{1,0:T(8,128)S(1)} %get-tuple-element.16), channel_id=1, source_target_pairs={{0,2},{1,3},{2,4},{3,5},{4,6},{5,7},{6,8},{7,9},{8,10},{9,11},{10,... | collective-permute-start | bytes 294920 | tf_op jit(solution)/shard_map/ppermute | solution.py:151
  50.2 0.0 collective-permute-done.2.refs_0_
  50.2 5.8 %pairs1.5 = (f32[16,1536]{1,0:T(8,128)S(1)}, f32[16,1536]{1,0:T(8,128)S(1)}) custom-call(bf16[1536,64]{1,0:T(8,128)(2,1)S(1)} %get-tuple-element.11.left_ref, bf16[32,1536]{1,0:T(8,128)(2,1)S(1)} %get-tuple-element.12.sides_ref, f32[24,1536]{1,0:T(8,128)S(1)} %collective-permute-done.2.refs_0_), custom_call_target="tpu_custom_call" | custom-call | flops 6000000000 | bytes 600000 | tf_op jit(solution)/shard_map/pairs1/pallas_call | solution.py:141
  56.0 2.1 %collective-permute-start.5 = (f32[16,1536]{1,0:T(8,128)S(1)}, f32[16,1536]{1,0:T(8,128)S(1)}, u32[]{:S(2)}, u32[]{:S(2)}) collective-permute-start(f32[16,1536]{1,0:T(8,128)S(1)} %get-tuple-element.18), channel_id=1, source_target_pairs={{0,1023},{1,0},{2,1},{3,2},{4,3},{5,4},{6,5},{7,6},{8,7},{9,8},{10... | collective-permute-start | bytes 294920 | tf_op jit(solution)/shard_map/ppermute | solution.py:151
  58.1 0.0 copy-start.4
  58.1 3.7 %own.1 = f32[16,1536]{1,0:T(8,128)S(1)} custom-call(bf16[1536,64]{1,0:T(8,128)(2,1)S(1)} %get-tuple-element.11.left_ref, bf16[32,1536]{1,0:T(8,128)(2,1)S(1)} %get-tuple-element.12.sides_ref, f32[24,1536]{1,0:T(8,128)S(1)} %pad_maximum_fusion.packed_ref.own_ref), custom_call_target="tpu_custom_call" | custom-call | flops 4000000000 | bytes 600000 | tf_op jit(solution)/shard_map/own/pallas_call | solution.py:145
  61.7 0.0 collective-permute-done.4
  61.8 0.0 collective-permute-done.3
  61.8 0.3 collective-permute-done.5
  62.1 0.0 copy-done
  62.1 0.0 copy-done.1
  62.1 0.0 copy-done.4
  62.1 0.2 multiply_reduce_fusion.3
  62.3 0.1 pad_maximum_fusion.1
  62.4 21.5 %all_to_all.12 = f32[32,1,64]{2,1,0:T(1,128)S(1)} all-to-all(f32[32,1,64]{2,1,0:T(1,128)S(1)} %broadcast_in_dim.4), channel_id=1, replica_groups=mesh['hi'=32,'lo'=32] {'lo'}, dimensions={0} | all-to-all | bytes 16384 | tf_op jit(solution)/shard_map/all_to_all | solution.py:158
  83.9 14.6 %all_to_all.13 = f32[32,1,64]{2,1,0:T(1,128)S(1)} all-to-all(f32[32,1,64]{2,1,0:T(1,128)S(1)} %broadcast_in_dim.5), channel_id=1, replica_groups=mesh['hi'=32,'lo'=32] {'hi'}, dimensions={0} | all-to-all | bytes 16384 | tf_op jit(solution)/shard_map/all_to_all | solution.py:158
  98.6 0.1 maximum_divide_fusion
  98.7 0.0 copy-done.2
  98.7 0.8 multiply_add_fusion
  (9 shorter events, 0.1 us)
Async XLA Ops:
  1.3 0.9 copy-start.3
  2.3 29.9 %collective-permute-start.1 = (f32[24,1536]{1,0:T(8,128)S(1)}, f32[24,1536]{1,0:T(8,128)S(1)}, u32[]{:S(2)}, u32[]{:S(2)}) collective-permute-start(f32[24,1536]{1,0:T(8,128)S(1)} %pad_maximum_fusion.packed_ref.own_ref), channel_id=1, source_target_pairs={{0,3},{1,4},{2,5},{3,6},{4,7},{5,8},{6,9},{7,10},{8,11},{9,12},{10... | collective-permute-start | bytes 442376 | tf_op jit(solution)/shard_map/ppermute | solution.py:151
  9.5 40.7 %collective-permute-start.2 = (f32[24,1536]{1,0:T(8,128)S(1)}, f32[24,1536]{1,0:T(8,128)S(1)}, u32[]{:S(2)}, u32[]{:S(2)}) collective-permute-start(f32[24,1536]{1,0:T(8,128)S(1)} %pad_maximum_fusion.packed_ref.own_ref), channel_id=1, source_target_pairs={{0,1},{1,2},{2,3},{3,4},{4,5},{5,6},{6,7},{7,8},{8,9},{9,10},{10,1... | collective-permute-start | bytes 442376 | tf_op jit(solution)/shard_map/ppermute | solution.py:151
  11.4 30.8 %collective-permute-start = (f32[24,1536]{1,0:T(8,128)S(1)}, f32[24,1536]{1,0:T(8,128)S(1)}, u32[]{:S(2)}, u32[]{:S(2)}) collective-permute-start(f32[24,1536]{1,0:T(8,128)S(1)} %pad_maximum_fusion.packed_ref.own_ref), channel_id=1, source_target_pairs={{0,1022},{1,1023},{2,0},{3,1},{4,2},{5,3},{6,4},{7,5},{8,6},{9,7},... | collective-permute-start | bytes 442376 | tf_op jit(solution)/shard_map/ppermute | solution.py:151
  38.0 23.7 %collective-permute-start.4 = (f32[16,1536]{1,0:T(8,128)S(1)}, f32[16,1536]{1,0:T(8,128)S(1)}, u32[]{:S(2)}, u32[]{:S(2)}) collective-permute-start(f32[16,1536]{1,0:T(8,128)S(1)} %get-tuple-element.17), channel_id=1, source_target_pairs={{0,1021},{1,1022},{2,1023},{3,0},{4,1},{5,2},{6,3},{7,4},{8,5},{9,... | collective-permute-start | bytes 294920 | tf_op jit(solution)/shard_map/ppermute | solution.py:151
  48.1 13.7 %collective-permute-start.3 = (f32[16,1536]{1,0:T(8,128)S(1)}, f32[16,1536]{1,0:T(8,128)S(1)}, u32[]{:S(2)}, u32[]{:S(2)}) collective-permute-start(f32[16,1536]{1,0:T(8,128)S(1)} %get-tuple-element.16), channel_id=1, source_target_pairs={{0,2},{1,3},{2,4},{3,5},{4,6},{5,7},{6,8},{7,9},{8,10},{9,11},{10,... | collective-permute-start | bytes 294920 | tf_op jit(solution)/shard_map/ppermute | solution.py:151
  56.0 6.1 %copy-start = (f32[16,1536]{1,0:T(8,128)S(1)}, f32[16,1536]{1,0:T(8,128)}, u32[]{:S(2)}) copy-start(f32[16,1536]{1,0:T(8,128)} %param.11) | copy-start | bytes 294916
  56.0 6.1 %copy-start.1 = (f32[16,1536]{1,0:T(8,128)S(1)}, f32[16,1536]{1,0:T(8,128)}, u32[]{:S(2)}) copy-start(f32[16,1536]{1,0:T(8,128)} %param.10) | copy-start | bytes 294916
  56.0 6.1 %collective-permute-start.5 = (f32[16,1536]{1,0:T(8,128)S(1)}, f32[16,1536]{1,0:T(8,128)S(1)}, u32[]{:S(2)}, u32[]{:S(2)}) collective-permute-start(f32[16,1536]{1,0:T(8,128)S(1)} %get-tuple-element.18), channel_id=1, source_target_pairs={{0,1023},{1,0},{2,1},{3,2},{4,3},{5,4},{6,5},{7,6},{8,7},{9,8},{10... | collective-permute-start | bytes 294920 | tf_op jit(solution)/shard_map/ppermute | solution.py:151
  58.1 4.0 %copy-start.4 = (f32[1536]{0:T(1024)S(1)}, f32[1536]{0:T(1024)}, u32[]{:S(2)}) copy-start(f32[1536]{0:T(1024)} %param.8) | copy-start | bytes 18436
  62.3 36.4 %copy-start.2 = (f32[16,1536]{1,0:T(8,128)S(1)}, f32[16,1536]{1,0:T(8,128)}, u32[]{:S(2)}) copy-start(f32[16,1536]{1,0:T(8,128)} %param.9) | copy-start | bytes 294916

commit v4 on v1

--- a/solution.py
+++ b/solution.py
@@ -77,28 +77,35 @@
     return both[:rows] + both[rows:] + dot(sides[:rows], low)
 
 
-def prepare_body(coords_ref, inv_ref, dir_ref, packed_ref, left_ref, sides_ref):
-    scaled = coords_ref[...] * (inv_ref[...] * COORD_SCALE)
-    weighted = dir_ref[...] * SCALE
-    packed_ref[0:8, :] = scaled
-    packed_ref[8:24, :] = weighted
-    left_ref[...] = features(scaled, True).T.astype(bf16)
-    sides_ref[...] = stacked(weighted)
-
-
-def pair_body(left_ref, sides_ref, far_ref, near_ref, back_ref):
+def prepare_body(packed_ref, left_ref, sides_ref):
+    left_ref[...] = features(packed_ref[0:8, :], True).T.astype(bf16)
+    sides_ref[...] = stacked(packed_ref[8:24, :])
+
+
+def block_products(left, sides, far_ref, base_ref, near_ref, back_ref):
     sites = far_ref.shape[1]
     right = features(far_ref[0:8, :], False).astype(bf16)
     far_sides = stacked(far_ref[8:24, :])
     near = None
     for start in range(0, sites, TILE):
         columns = slice(start, start + TILE)
-        values = covariance(product(left_ref[...], right[:, columns]))
+        values = covariance(product(left, right[:, columns]))
         high, low = split2(values)
         part = applied(product_t, far_sides[:, columns], high, low)
         near = part if near is None else near + part
-        back_ref[:, columns] = applied(product, sides_ref[...], high, low)
+        back = applied(product, sides, high, low)
+        back_ref[:, columns] = back if base_ref is None else back + base_ref[:, columns]
     near_ref[...] = near
+
+
+def own_pair_body(left_ref, sides_ref, far_ref, *refs):
+    base_ref = refs[0] if len(refs) == 3 else None
+    block_products(left_ref[...], sides_ref[...], far_ref, base_ref, refs[-2], refs[-1])
+
+
+def far_pair_body(one_ref, other_ref, base_ref, near_ref, back_ref):
+    left = features(one_ref[0:8, :], True).T.astype(bf16)
+    block_products(left, stacked(one_ref[8:24, :]), other_ref, base_ref, near_ref, back_ref)
 
 
 def self_body(left_ref, sides_ref, own_ref, out_ref):
@@ -129,15 +136,20 @@
     return jax.ShapeDtypeStruct((rows, columns), dtype)
 
 
-def prepare(coords, inv_scale, direction):
-    sites, rhs = coords.shape[1], direction.shape[0]
-    shapes = (shape(8 + rhs, sites), shape(sites, 64, bf16), shape(2 * rhs, sites, bf16))
-    return call(prepare_body, "prepare", shapes, 10**7)(coords, inv_scale[:, None], direction)
-
-
-def pair(left, sides, far):
+def prepare(packed):
+    rows, sites = packed.shape
+    shapes = (shape(sites, 64, bf16), shape(2 * (rows - 8), sites, bf16))
+    return call(prepare_body, "prepare", shapes, 10**7)(packed)
+
+
+def own_pair(left, sides, far, *base):
     out = shape(16, far.shape[1])
-    return call(pair_body, "pair", (out, out), 6 * 10**9)(left, sides, far)
+    return call(own_pair_body, "own_pair", (out, out), 6 * 10**9)(left, sides, far, *base)
+
+
+def far_pair(one, other, base):
+    out = shape(16, one.shape[1])
+    return call(far_pair_body, "far_pair", (out, out), 6 * 10**9)(one, other, base)
 
 
 def own_block(left, sides, packed):
@@ -160,18 +172,18 @@
 
 def local(coords, inv_scale, noise_var, solution, residual, direction):
     rhs = direction.shape[0]
-    packed, left, sides = prepare(coords, inv_scale, direction)
-    gp_image = noise_var[None, :] * direction
-    fars = [shifted(packed, offset) for offset in range(1, ROUNDS + 1)]
-    returns = []
-    for offset, far in zip(range(1, ROUNDS + 1), fars):
-        near, back = pair(left, sides, far)
-        gp_image = gp_image + near
-        returns.append(shifted(back, -offset))
+    scaled = (coords * COORD_SCALE) * inv_scale[:, None]
+    packed = jnp.concatenate([scaled, direction * SCALE], axis=0)
+    right = shifted(packed, -1)
+    left2 = shifted(packed, 2)
+    left, sides = prepare(packed)
+    near_right, to_right = own_pair(left, sides, right)
+    to_left2, to_right = far_pair(left2, right, to_right)
+    from_left = shifted(to_right, 1)
+    near_left2, to_left2 = own_pair(left, sides, left2, to_left2)
+    from_right2 = shifted(to_left2, -2)
     own = own_block(left, sides, packed)
-    gp_image = gp_image + (2.0 * ROUNDS) * own
-    for back in returns:
-        gp_image = gp_image + back
+    gp_image = noise_var[None, :] * direction + near_right + near_left2 + (2.0 * ROUNDS) * own + from_left + from_right2
     sums = [
         jnp.sum(residual * residual, axis=1),
         jnp.sum(direction * gp_image, axis=1),

time: 96.6 us -> 95.2 us (0.986)
  waiting for transfers between devices: 16.2 us -> 4.98 us
  starting transfers between devices: 23.3 us -> 32.7 us
  local copies, waits for them, and re-layouts: 2.46 us -> 0.06 us
  other arithmetic: 1.22 us -> 2.85 us
    ppermute x6 -> x4, waiting for transfers between devices: 16.2 us -> 4.98 us  [shifted(): return lax.ppermute(value, AXES, pairs)]
    ppermute x6 -> x4, starting transfers between devices: 23.3 us -> 32.7 us  [shifted(): return lax.ppermute(value, AXES, pairs)]
    unnamed x14 -> x10, local copies, waits for them, and re-layouts: 2.36 us -> 0.04 us
    mul x0 -> x3, other arithmetic: none -> 1.64 us  [the longest x1 0.91 us: local(): packed = jnp.concatenate([scaled, direction * SCALE], axis=0)]
  transfers between devices with their start and end apart: 6 -> 4, of which waited for: 1 -> 1; matrix products, arithmetic and copies ran while one was open for 0% -> 0% of each run, Pallas kernels for 22% -> 10%
where the time goes in v4:
time: 95.2 us; the launch traced here: 94.9 us
  starting transfers between devices  32.7 us (34%)
  blocking collectives  31.8 us (33%)
  Pallas kernels  21.7 us (23%)
  waiting for transfers between devices  4.98 us (5%)
  other arithmetic  2.85 us (3%)
    ppermute x4, starting transfers between devices, shifted(): return lax.ppermute(value, AXES, pairs)  32.7 us
    all_to_all x2, blocking collectives, total(): values = jnp.sum(lax.all_to_all(copies, axis, 0, 0, tiled=True), axis=0)  31.8 us
    pallas_call x2, Pallas kernels, own_pair(): call(own_pair_body, 'own_pair', (out, out), 6 * 10 ** 9)  11.8 us
    pallas_call x1, Pallas kernels, far_pair(): call(far_pair_body, 'far_pair', (out, out), 6 * 10 ** 9)(one, other, base)  6.06 us
    ppermute x4, waiting for transfers between devices, shifted(): return lax.ppermute(value, AXES, pairs)  4.98 us
    pallas_call x1, Pallas kernels, own_block(): call(self_body, 'own', shape(16, packed.shape[1]), 4 * 10 ** 9)  3.66 us
  transfers between devices with their start and end apart: 4, of which 1 were waited for; matrix products, arithmetic and copies ran while one was open for 0% of the time, Pallas kernels for 10%

profile of v4, /device:TPU:1, one launch (start us, length us, event | category | flops | bytes accessed | tf_op | source)
XLA Modules:
  0.0 94.9 jit_solution(7549890373125073994)
XLA Ops:
  0.6 0.7 broadcast_multiply_fusion.2
  1.3 0.0 copy-start.3
  1.3 0.9 broadcast_multiply_fusion
  2.2 0.0 copy-done.3
  2.2 0.1 broadcast_multiply_fusion.1
  2.3 16.1 %collective-permute-start = (f32[24,1536]{1,0:T(8,128)S(1)}, f32[24,1536]{1,0:T(8,128)S(1)}, u32[]{:S(2)}, u32[]{:S(2)}) collective-permute-start(f32[24,1536]{1,0:T(8,128)S(1)} %pad_maximum_fusion.packed_ref.own_ref), channel_id=1, source_target_pairs={{0,1023},{1,0},{2,1},{3,2},{4,3},{5,4},{6,5},{7,6},{8,7},{9,8},{10... | collective-permute-start | bytes 442376 | tf_op jit(solution)/shard_map/ppermute | solution.py:162
  18.4 1.9 %collective-permute-start.1 = (f32[24,1536]{1,0:T(8,128)S(1)}, f32[24,1536]{1,0:T(8,128)S(1)}, u32[]{:S(2)}, u32[]{:S(2)}) collective-permute-start(f32[24,1536]{1,0:T(8,128)S(1)} %pad_maximum_fusion.packed_ref.own_ref), channel_id=1, source_target_pairs={{0,2},{1,3},{2,4},{3,5},{4,6},{5,7},{6,8},{7,9},{8,10},{9,11},{10,... | collective-permute-start | bytes 442376 | tf_op jit(solution)/shard_map/ppermute | solution.py:162
  20.3 0.2 prepare.1
  20.5 0.0 collective-permute-done.far_ref.other_ref
  20.5 5.8 %own_pair.2 = (f32[16,1536]{1,0:T(8,128)S(1)}, f32[16,1536]{1,0:T(8,128)S(1)}) custom-call(bf16[1536,64]{1,0:T(8,128)(2,1)S(1)} %get-tuple-element.11.left_ref, bf16[32,1536]{1,0:T(8,128)(2,1)S(1)} %get-tuple-element.12.sides_ref, f32[24,1536]{1,0:T(8,128)S(1)} %collective-permute-done.far_ref.other_ref), custom_call_target="tpu_custom_call" | custom-call | flops 6000000000 | bytes 600000 | tf_op jit(solution)/shard_map/own_pair/pallas_call | solution.py:147
  26.3 5.0 %collective-permute-done.1.one_ref.far_ref = f32[24,1536]{1,0:T(8,128)S(1)} collective-permute-done((f32[24,1536]{1,0:T(8,128)S(1)}, f32[24,1536]{1,0:T(8,128)S(1)}, u32[]{:S(2)}, u32[]{:S(2)}) %collective-permute-start.1) | collective-permute-done | bytes 147488 | tf_op jit(solution)/shard_map/ppermute | solution.py:162
  31.3 6.1 %far_pair.1 = (f32[16,1536]{1,0:T(8,128)S(1)}, f32[16,1536]{1,0:T(8,128)S(1)}) custom-call(f32[24,1536]{1,0:T(8,128)S(1)} %collective-permute-done.1.one_ref.far_ref, f32[24,1536]{1,0:T(8,128)S(1)} %collective-permute-done.far_ref.other_ref, f32[16,1536]{1,0:T(8,128)S(1)} %get-tuple-element.14.base_ref), custom_call_target="tpu_custom_call" | custom-call | flops 6000000000 | bytes 600000 | tf_op jit(solution)/shard_map/far_pair/pallas_call | solution.py:152
  37.4 6.0 %own_pair.3 = (f32[16,1536]{1,0:T(8,128)S(1)}, f32[16,1536]{1,0:T(8,128)S(1)}) custom-call(bf16[1536,64]{1,0:T(8,128)(2,1)S(1)} %get-tuple-element.11.left_ref, bf16[32,1536]{1,0:T(8,128)(2,1)S(1)} %get-tuple-element.12.sides_ref, f32[24,1536]{1,0:T(8,128)S(1)} %collective-permute-done.1.one_ref.far_ref, f32[16,1536]{1,0:T(8,128)S(1)} %get-tuple-element.15.refs_0_), custom_call_target="tpu_custom_call" | custom-call | flops 6000000000 | bytes 600000 | tf_op jit(solution)/shard_map/own_pair/pallas_call | solution.py:147
  43.4 12.6 %collective-permute-start.3 = (f32[16,1536]{1,0:T(8,128)S(1)}, f32[16,1536]{1,0:T(8,128)S(1)}, u32[]{:S(2)}, u32[]{:S(2)}) collective-permute-start(f32[16,1536]{1,0:T(8,128)S(1)} %get-tuple-element.18), channel_id=1, source_target_pairs={{0,1022},{1,1023},{2,0},{3,1},{4,2},{5,3},{6,4},{7,5},{8,6},{9,7},... | collective-permute-start | bytes 294920 | tf_op jit(solution)/shard_map/ppermute | solution.py:162
  56.0 0.0 copy-start
  56.0 0.0 copy-start.1
  56.0 2.1 %collective-permute-start.2 = (f32[16,1536]{1,0:T(8,128)S(1)}, f32[16,1536]{1,0:T(8,128)S(1)}, u32[]{:S(2)}, u32[]{:S(2)}) collective-permute-start(f32[16,1536]{1,0:T(8,128)S(1)} %get-tuple-element.17), channel_id=1, source_target_pairs={{0,1},{1,2},{2,3},{3,4},{4,5},{5,6},{6,7},{7,8},{8,9},{9,10},{10,1... | collective-permute-start | bytes 294920 | tf_op jit(solution)/shard_map/ppermute | solution.py:162
  58.1 0.0 copy-start.4
  58.1 3.7 %own.1 = f32[16,1536]{1,0:T(8,128)S(1)} custom-call(bf16[1536,64]{1,0:T(8,128)(2,1)S(1)} %get-tuple-element.11.left_ref, bf16[32,1536]{1,0:T(8,128)(2,1)S(1)} %get-tuple-element.12.sides_ref, f32[24,1536]{1,0:T(8,128)S(1)} %pad_maximum_fusion.packed_ref.own_ref), custom_call_target="tpu_custom_call" | custom-call | flops 4000000000 | bytes 600000 | tf_op jit(solution)/shard_map/own/pallas_call | solution.py:156
  61.7 0.0 collective-permute-done.3
  61.7 0.0 collective-permute-done.2
  61.7 0.0 copy-done
  61.8 0.0 copy-done.1
  61.8 0.0 copy-done.4
  61.8 0.2 multiply_reduce_fusion.3
  62.0 0.0 copy-start.2
  62.0 0.1 pad_maximum_fusion.1
  62.1 20.2 %all_to_all.12 = f32[32,1,64]{2,1,0:T(1,128)S(1)} all-to-all(f32[32,1,64]{2,1,0:T(1,128)S(1)} %broadcast_in_dim.4), channel_id=1, replica_groups=mesh['hi'=32,'lo'=32] {'lo'}, dimensions={0} | all-to-all | bytes 16384 | tf_op jit(solution)/shard_map/all_to_all | solution.py:169
  82.3 11.6 %all_to_all.13 = f32[32,1,64]{2,1,0:T(1,128)S(1)} all-to-all(f32[32,1,64]{2,1,0:T(1,128)S(1)} %broadcast_in_dim.5), channel_id=1, replica_groups=mesh['hi'=32,'lo'=32] {'hi'}, dimensions={0} | all-to-all | bytes 16384 | tf_op jit(solution)/shard_map/all_to_all | solution.py:169
  94.0 0.1 maximum_divide_fusion
  94.1 0.0 copy-done.2
  94.1 0.8 multiply_add_fusion
  (5 shorter events, 0.1 us)
Async XLA Ops:
  1.3 0.9 copy-start.3
  2.3 18.2 %collective-permute-start = (f32[24,1536]{1,0:T(8,128)S(1)}, f32[24,1536]{1,0:T(8,128)S(1)}, u32[]{:S(2)}, u32[]{:S(2)}) collective-permute-start(f32[24,1536]{1,0:T(8,128)S(1)} %pad_maximum_fusion.packed_ref.own_ref), channel_id=1, source_target_pairs={{0,1023},{1,0},{2,1},{3,2},{4,3},{5,4},{6,5},{7,6},{8,7},{9,8},{10... | collective-permute-start | bytes 442376 | tf_op jit(solution)/shard_map/ppermute | solution.py:162
  18.4 12.9 %collective-permute-start.1 = (f32[24,1536]{1,0:T(8,128)S(1)}, f32[24,1536]{1,0:T(8,128)S(1)}, u32[]{:S(2)}, u32[]{:S(2)}) collective-permute-start(f32[24,1536]{1,0:T(8,128)S(1)} %pad_maximum_fusion.packed_ref.own_ref), channel_id=1, source_target_pairs={{0,2},{1,3},{2,4},{3,5},{4,6},{5,7},{6,8},{7,9},{8,10},{9,11},{10,... | collective-permute-start | bytes 442376 | tf_op jit(solution)/shard_map/ppermute | solution.py:162
  43.4 18.4 %collective-permute-start.3 = (f32[16,1536]{1,0:T(8,128)S(1)}, f32[16,1536]{1,0:T(8,128)S(1)}, u32[]{:S(2)}, u32[]{:S(2)}) collective-permute-start(f32[16,1536]{1,0:T(8,128)S(1)} %get-tuple-element.18), channel_id=1, source_target_pairs={{0,1022},{1,1023},{2,0},{3,1},{4,2},{5,3},{6,4},{7,5},{8,6},{9,7},... | collective-permute-start | bytes 294920 | tf_op jit(solution)/shard_map/ppermute | solution.py:162
  56.0 5.8 %copy-start = (f32[16,1536]{1,0:T(8,128)S(1)}, f32[16,1536]{1,0:T(8,128)}, u32[]{:S(2)}) copy-start(f32[16,1536]{1,0:T(8,128)} %param.11) | copy-start | bytes 294916
  56.0 5.8 %copy-start.1 = (f32[16,1536]{1,0:T(8,128)S(1)}, f32[16,1536]{1,0:T(8,128)}, u32[]{:S(2)}) copy-start(f32[16,1536]{1,0:T(8,128)} %param.10) | copy-start | bytes 294916
  56.0 5.7 %collective-permute-start.2 = (f32[16,1536]{1,0:T(8,128)S(1)}, f32[16,1536]{1,0:T(8,128)S(1)}, u32[]{:S(2)}, u32[]{:S(2)}) collective-permute-start(f32[16,1536]{1,0:T(8,128)S(1)} %get-tuple-element.17), channel_id=1, source_target_pairs={{0,1},{1,2},{2,3},{3,4},{4,5},{5,6},{6,7},{7,8},{8,9},{9,10},{10,1... | collective-permute-start | bytes 294920 | tf_op jit(solution)/shard_map/ppermute | solution.py:162
  58.1 3.7 %copy-start.4 = (f32[1536]{0:T(1024)S(1)}, f32[1536]{0:T(1024)}, u32[]{:S(2)}) copy-start(f32[1536]{0:T(1024)} %param.8) | copy-start | bytes 18436
  62.0 32.1 %copy-start.2 = (f32[16,1536]{1,0:T(8,128)S(1)}, f32[16,1536]{1,0:T(8,128)}, u32[]{:S(2)}) copy-start(f32[16,1536]{1,0:T(8,128)} %param.9) | copy-start | bytes 294916

commit v5 on v4

--- a/solution.py
+++ b/solution.py
@@ -77,15 +77,23 @@
     return both[:rows] + both[rows:] + dot(sides[:rows], low)
 
 
-def prepare_body(packed_ref, left_ref, sides_ref):
-    left_ref[...] = features(packed_ref[0:8, :], True).T.astype(bf16)
-    sides_ref[...] = stacked(packed_ref[8:24, :])
-
-
-def block_products(left, sides, far_ref, base_ref, near_ref, back_ref):
+def left_side(packed_ref, inv_ref):
+    scaled = packed_ref[0:8, :] * (inv_ref[...] * COORD_SCALE)
+    return features(scaled, True).T.astype(bf16), stacked(packed_ref[8:24, :] * SCALE)
+
+
+def right_side(packed_ref, inv_ref):
+    scaled = packed_ref[0:8, :] * (inv_ref[...] * COORD_SCALE)
+    return features(scaled, False).astype(bf16), stacked(packed_ref[8:24, :] * SCALE)
+
+
+def prepare_body(packed_ref, inv_ref, left_ref, sides_ref):
+    left_ref[...], sides_ref[...] = left_side(packed_ref, inv_ref)
+
+
+def block_products(left, sides, far_ref, inv_ref, base_ref, near_ref, back_ref):
     sites = far_ref.shape[1]
-    right = features(far_ref[0:8, :], False).astype(bf16)
-    far_sides = stacked(far_ref[8:24, :])
+    right, far_sides = right_side(far_ref, inv_ref)
     near = None
     for start in range(0, sites, TILE):
         columns = slice(start, start + TILE)
@@ -98,19 +106,19 @@
     near_ref[...] = near
 
 
-def own_pair_body(left_ref, sides_ref, far_ref, *refs):
+def own_pair_body(left_ref, sides_ref, far_ref, inv_ref, *refs):
     base_ref = refs[0] if len(refs) == 3 else None
-    block_products(left_ref[...], sides_ref[...], far_ref, base_ref, refs[-2], refs[-1])
-
-
-def far_pair_body(one_ref, other_ref, base_ref, near_ref, back_ref):
-    left = features(one_ref[0:8, :], True).T.astype(bf16)
-    block_products(left, stacked(one_ref[8:24, :]), other_ref, base_ref, near_ref, back_ref)
-
-
-def self_body(left_ref, sides_ref, own_ref, out_ref):
+    block_products(left_ref[...], sides_ref[...], far_ref, inv_ref, base_ref, refs[-2], refs[-1])
+
+
+def far_pair_body(one_ref, other_ref, inv_ref, base_ref, near_ref, back_ref):
+    left, sides = left_side(one_ref, inv_ref)
+    block_products(left, sides, other_ref, inv_ref, base_ref, near_ref, back_ref)
+
+
+def self_body(left_ref, sides_ref, own_ref, inv_ref, base_ref, out_ref):
     sites = own_ref.shape[1]
-    right = features(own_ref[0:8, :], False).astype(bf16)
+    right, _ = right_side(own_ref, inv_ref)
     out_ref[...] = jnp.zeros_like(out_ref)
     for start in range(0, sites, TILE):
         stop = start + TILE
@@ -120,6 +128,7 @@
         out_ref[:, 0:stop] += applied(product_t, sides_ref[:, columns], high, low)
         if start:
             out_ref[:, columns] += applied(product, sides_ref[:, 0:start], high[0:start], low[0:start])
+    out_ref[...] = (2.0 * ROUNDS) * out_ref[...] + base_ref[...]
 
 
 def call(body, name, shapes, cost):
@@ -136,24 +145,24 @@
     return jax.ShapeDtypeStruct((rows, columns), dtype)
 
 
-def prepare(packed):
+def prepare(packed, inv):
     rows, sites = packed.shape
     shapes = (shape(sites, 64, bf16), shape(2 * (rows - 8), sites, bf16))
-    return call(prepare_body, "prepare", shapes, 10**7)(packed)
-
-
-def own_pair(left, sides, far, *base):
+    return call(prepare_body, "prepare", shapes, 10**7)(packed, inv)
+
+
+def own_pair(left, sides, far, inv, *base):
     out = shape(16, far.shape[1])
-    return call(own_pair_body, "own_pair", (out, out), 6 * 10**9)(left, sides, far, *base)
-
-
-def far_pair(one, other, base):
+    return call(own_pair_body, "own_pair", (out, out), 6 * 10**9)(left, sides, far, inv, *base)
+
+
+def far_pair(one, other, inv, base):
     out = shape(16, one.shape[1])
-    return call(far_pair_body, "far_pair", (out, out), 6 * 10**9)(one, other, base)
-
-
-def own_block(left, sides, packed):
-    return call(self_body, "own", shape(16, packed.shape[1]), 4 * 10**9)(left, sides, packed)
+    return call(far_pair_body, "far_pair", (out, out), 6 * 10**9)(one, other, inv, base)
+
+
+def own_block(left, sides, packed, inv, base):
+    return call(self_body, "own", shape(16, packed.shape[1]), 4 * 10**9)(left, sides, packed, inv, base)
 
 
 def shifted(value, steps):
@@ -172,18 +181,18 @@
 
 def local(coords, inv_scale, noise_var, solution, residual, direction):
     rhs = direction.shape[0]
-    scaled = (coords * COORD_SCALE) * inv_scale[:, None]
-    packed = jnp.concatenate([scaled, direction * SCALE], axis=0)
+    packed = jnp.concatenate([coords, direction], axis=0)
+    inv = inv_scale[:, None]
     right = shifted(packed, -1)
     left2 = shifted(packed, 2)
-    left, sides = prepare(packed)
-    near_right, to_right = own_pair(left, sides, right)
-    to_left2, to_right = far_pair(left2, right, to_right)
+    left, sides = prepare(packed, inv)
+    near_right, to_right = own_pair(left, sides, right, inv)
+    to_left2, to_right = far_pair(left2, right, inv, to_right)
     from_left = shifted(to_right, 1)
-    near_left2, to_left2 = own_pair(left, sides, left2, to_left2)
+    near_left2, to_left2 = own_pair(left, sides, left2, inv, to_left2)
     from_right2 = shifted(to_left2, -2)
-    own = own_block(left, sides, packed)
-    gp_image = noise_var[None, :] * direction + near_right + near_left2 + (2.0 * ROUNDS) * own + from_left + from_right2
+    own = own_block(left, sides, packed, inv, from_left)
+    gp_image = noise_var[None, :] * direction + near_right + near_left2 + own + from_right2
     sums = [
         jnp.sum(residual * residual, axis=1),
         jnp.sum(direction * gp_image, axis=1),

time: 95.2 us -> 95.6 us (level)
  starting transfers between devices: 32.7 us -> 36.7 us
  blocking collectives: 31.8 us -> 28.9 us
  other arithmetic: 2.85 us -> 1.2 us
  local copies, waits for them, and re-layouts: 0.06 us -> 1.06 us
    ppermute x4, starting transfers between devices: 32.7 us -> 36.7 us  [shifted(): return lax.ppermute(value, AXES, pairs)]
    all_to_all x2, blocking collectives: 31.8 us -> 28.9 us  [total(): values = jnp.sum(lax.all_to_all(copies, axis, 0, 0, tiled=True), axis=0)]
    mul x3 -> x0, other arithmetic: 1.64 us -> none  [the longest x1 0.91 us: local(): packed = jnp.concatenate([scaled, direction * SCALE], axis=0)]
  transfers between devices with their start and end apart: 4 -> 4, of which waited for: 1 -> 1; matrix products, arithmetic and copies ran while one was open for 0% -> 0% of each run, Pallas kernels for 10% -> 17%
where the time goes in v5:
time: 95.6 us; the launch traced here: 95.2 us
  starting transfers between devices  36.7 us (38%)
  blocking collectives  28.9 us (30%)
  Pallas kernels  22 us (23%)
  waiting for transfers between devices  4.71 us (5%)
  other arithmetic  1.2 us (1%)
  local copies, waits for them, and re-layouts  1.06 us (1%)
    ppermute x4, starting transfers between devices, shifted(): return lax.ppermute(value, AXES, pairs)  36.7 us
    all_to_all x2, blocking collectives, total(): values = jnp.sum(lax.all_to_all(copies, axis, 0, 0, tiled=True), axis=0)  28.9 us
    pallas_call x2, Pallas kernels, own_pair(): call(own_pair_body, 'own_pair', (out, out), 6 * 10 ** 9)  11.9 us
    pallas_call x1, Pallas kernels, far_pair(): call(far_pair_body, 'far_pair', (out, out), 6 * 10 ** 9)  6.11 us
    ppermute x4, waiting for transfers between devices, shifted(): return lax.ppermute(value, AXES, pairs)  4.71 us
    pallas_call x1, Pallas kernels, own_block(): call(self_body, 'own', shape(16, packed.shape[1]), 4 * 10 ** 9)  3.75 us
  transfers between devices with their start and end apart: 4, of which 1 were waited for; matrix products, arithmetic and copies ran while one was open for 0% of the time, Pallas kernels for 17%

profile of v5, /device:TPU:1, one launch (start us, length us, event | category | flops | bytes accessed | tf_op | source)
XLA Modules:
  0.0 95.2 jit_solution(8642536867389627481)
XLA Ops:
  0.6 0.0 copy-start
  0.6 0.8 constant_dynamic-update-slice_fusion.1
  1.5 0.1 copy-done
  1.6 0.0 copy-start.4
  1.6 16.1 %collective-permute-start = (f32[24,1536]{1,0:T(8,128)S(1)}, f32[24,1536]{1,0:T(8,128)S(1)}, u32[]{:S(2)}, u32[]{:S(2)}) collective-permute-start(f32[24,1536]{1,0:T(8,128)S(1)} %constant_dynamic-update-slice_fusion.packed_ref.own_ref), channel_id=1, source_target_pairs={{0,1023},{1,0},{2,1},{3,2},{4,3},{5,4},{6,5},{7,6},{8,7},{9,8},{10... | collective-permute-start | bytes 442376 | tf_op jit(solution)/shard_map/ppermute | solution.py:171
  17.6 1.9 %collective-permute-start.1 = (f32[24,1536]{1,0:T(8,128)S(1)}, f32[24,1536]{1,0:T(8,128)S(1)}, u32[]{:S(2)}, u32[]{:S(2)}) collective-permute-start(f32[24,1536]{1,0:T(8,128)S(1)} %constant_dynamic-update-slice_fusion.packed_ref.own_ref), channel_id=1, source_target_pairs={{0,2},{1,3},{2,4},{3,5},{4,6},{5,7},{6,8},{7,9},{8,10},{9,11},{10,... | collective-permute-start | bytes 442376 | tf_op jit(solution)/shard_map/ppermute | solution.py:171
  19.6 0.0 copy-done.4
  19.6 0.1 copy.19.inv_ref
  19.7 0.2 prepare.1
  19.9 0.0 collective-permute-done.far_ref.other_ref
  19.9 5.9 %own_pair.2 = (f32[16,1536]{1,0:T(8,128)S(1)}, f32[16,1536]{1,0:T(8,128)S(1)}) custom-call(bf16[1536,64]{1,0:T(8,128)(2,1)S(1)} %get-tuple-element.11.left_ref, bf16[32,1536]{1,0:T(8,128)(2,1)S(1)} %get-tuple-element.12.sides_ref, f32[24,1536]{1,0:T(8,128)S(1)} %collective-permute-done.far_ref.other_ref, f32[8,1]{1,0:T(8,128)S(1)} %copy.19.inv_ref), custom_call_target="tpu_custom_call" | custom-call | flops 6000000000 | bytes 600000 | tf_op jit(solution)/shard_map/own_pair/pallas_call | solution.py:156
  25.9 4.7 %collective-permute-done.1.one_ref.far_ref = f32[24,1536]{1,0:T(8,128)S(1)} collective-permute-done((f32[24,1536]{1,0:T(8,128)S(1)}, f32[24,1536]{1,0:T(8,128)S(1)}, u32[]{:S(2)}, u32[]{:S(2)}) %collective-permute-start.1) | collective-permute-done | bytes 147488 | tf_op jit(solution)/shard_map/ppermute | solution.py:171
  30.6 6.1 %far_pair.1 = (f32[16,1536]{1,0:T(8,128)S(1)}, f32[16,1536]{1,0:T(8,128)S(1)}) custom-call(f32[24,1536]{1,0:T(8,128)S(1)} %collective-permute-done.1.one_ref.far_ref, f32[24,1536]{1,0:T(8,128)S(1)} %collective-permute-done.far_ref.other_ref, f32[8,1]{1,0:T(8,128)S(1)} %copy.19.inv_ref, f32[16,1536]{1,0:T(8,128)S(1)} %get-tuple-element.14.base_ref), custom_call_target="tpu_custom_call" | custom-call | flops 6000000000 | bytes 600000 | tf_op jit(solution)/shard_map/far_pair/pallas_call | solution.py:161
  36.7 4.0 %collective-permute-start.2 = (f32[16,1536]{1,0:T(8,128)S(1)}, f32[16,1536]{1,0:T(8,128)S(1)}, u32[]{:S(2)}, u32[]{:S(2)}) collective-permute-start(f32[16,1536]{1,0:T(8,128)S(1)} %get-tuple-element.17), channel_id=1, source_target_pairs={{0,1},{1,2},{2,3},{3,4},{4,5},{5,6},{6,7},{7,8},{8,9},{9,10},{10,1... | collective-permute-start | bytes 294920 | tf_op jit(solution)/shard_map/ppermute | solution.py:171
  40.7 5.9 %own_pair.3 = (f32[16,1536]{1,0:T(8,128)S(1)}, f32[16,1536]{1,0:T(8,128)S(1)}) custom-call(bf16[1536,64]{1,0:T(8,128)(2,1)S(1)} %get-tuple-element.11.left_ref, bf16[32,1536]{1,0:T(8,128)(2,1)S(1)} %get-tuple-element.12.sides_ref, f32[24,1536]{1,0:T(8,128)S(1)} %collective-permute-done.1.one_ref.far_ref, f32[8,1]{1,0:T(8,128)S(1)} %copy.19.inv_ref, ...), custom_call_target="tpu_custom_call" | custom-call | flops 6000000000 | bytes 600000 | tf_op jit(solution)/shard_map/own_pair/pallas_call | solution.py:156
  46.6 0.0 copy-start.1
  46.7 14.6 %collective-permute-start.3 = (f32[16,1536]{1,0:T(8,128)S(1)}, f32[16,1536]{1,0:T(8,128)S(1)}, u32[]{:S(2)}, u32[]{:S(2)}) collective-permute-start(f32[16,1536]{1,0:T(8,128)S(1)} %get-tuple-element.18), channel_id=1, source_target_pairs={{0,1022},{1,1023},{2,0},{3,1},{4,2},{5,3},{6,4},{7,5},{8,6},{9,7},... | collective-permute-start | bytes 294920 | tf_op jit(solution)/shard_map/ppermute | solution.py:171
  61.3 0.0 collective-permute-done.2.base_ref
  61.3 0.0 copy-start.3
  61.3 3.7 %own.1 = f32[16,1536]{1,0:T(8,128)S(1)} custom-call(bf16[1536,64]{1,0:T(8,128)(2,1)S(1)} %get-tuple-element.11.left_ref, bf16[32,1536]{1,0:T(8,128)(2,1)S(1)} %get-tuple-element.12.sides_ref, f32[24,1536]{1,0:T(8,128)S(1)} %constant_dynamic-update-slice_fusion.packed_ref.own_ref, f32[8,1]{1,0:T(8,128)S(1)} %copy.19.inv_ref, ...), custom_call_target="tpu_custom_call" | custom-call | flops 4000000000 | bytes 600000 | tf_op jit(solution)/shard_map/own/pallas_call | solution.py:165
  65.1 0.0 collective-permute-done.3
  65.1 0.0 copy-done.1
  65.1 0.0 copy-done.3
  65.1 0.2 multiply_reduce_fusion.3
  65.3 0.0 copy-start.2
  65.3 0.1 pad_maximum_fusion
  65.4 13.5 %all_to_all.12 = f32[32,1,64]{2,1,0:T(1,128)S(1)} all-to-all(f32[32,1,64]{2,1,0:T(1,128)S(1)} %broadcast_in_dim.7), channel_id=1, replica_groups=mesh['hi'=32,'lo'=32] {'lo'}, dimensions={0} | all-to-all | bytes 16384 | tf_op jit(solution)/shard_map/all_to_all | solution.py:178
  79.0 15.3 %all_to_all.13 = f32[32,1,64]{2,1,0:T(1,128)S(1)} all-to-all(f32[32,1,64]{2,1,0:T(1,128)S(1)} %broadcast_in_dim.8), channel_id=1, replica_groups=mesh['hi'=32,'lo'=32] {'hi'}, dimensions={0} | all-to-all | bytes 16384 | tf_op jit(solution)/shard_map/all_to_all | solution.py:178
  94.3 0.1 maximum_divide_fusion
  94.4 0.0 copy-done.2
  94.4 0.8 multiply_add_fusion
  (5 shorter events, 0.1 us)
Async XLA Ops:
  0.6 0.9 copy-start
  1.6 18.0 %copy-start.4 = (f32[8]{0:T(128)S(1)}, f32[8]{0:T(128)}, u32[]{:S(2)}) copy-start(f32[8]{0:T(128)} %param.7) | copy-start | bytes 100
  1.6 18.3 %collective-permute-start = (f32[24,1536]{1,0:T(8,128)S(1)}, f32[24,1536]{1,0:T(8,128)S(1)}, u32[]{:S(2)}, u32[]{:S(2)}) collective-permute-start(f32[24,1536]{1,0:T(8,128)S(1)} %constant_dynamic-update-slice_fusion.packed_ref.own_ref), channel_id=1, source_target_pairs={{0,1023},{1,0},{2,1},{3,2},{4,3},{5,4},{6,5},{7,6},{8,7},{9,8},{10... | collective-permute-start | bytes 442376 | tf_op jit(solution)/shard_map/ppermute | solution.py:171
  17.6 12.9 %collective-permute-start.1 = (f32[24,1536]{1,0:T(8,128)S(1)}, f32[24,1536]{1,0:T(8,128)S(1)}, u32[]{:S(2)}, u32[]{:S(2)}) collective-permute-start(f32[24,1536]{1,0:T(8,128)S(1)} %constant_dynamic-update-slice_fusion.packed_ref.own_ref), channel_id=1, source_target_pairs={{0,2},{1,3},{2,4},{3,5},{4,6},{5,7},{6,8},{7,9},{8,10},{9,11},{10,... | collective-permute-start | bytes 442376 | tf_op jit(solution)/shard_map/ppermute | solution.py:171
  36.7 24.6 %collective-permute-start.2 = (f32[16,1536]{1,0:T(8,128)S(1)}, f32[16,1536]{1,0:T(8,128)S(1)}, u32[]{:S(2)}, u32[]{:S(2)}) collective-permute-start(f32[16,1536]{1,0:T(8,128)S(1)} %get-tuple-element.17), channel_id=1, source_target_pairs={{0,1},{1,2},{2,3},{3,4},{4,5},{5,6},{6,7},{7,8},{8,9},{9,10},{10,1... | collective-permute-start | bytes 294920 | tf_op jit(solution)/shard_map/ppermute | solution.py:171
  46.6 18.4 %copy-start.1 = (f32[16,1536]{1,0:T(8,128)S(1)}, f32[16,1536]{1,0:T(8,128)}, u32[]{:S(2)}) copy-start(f32[16,1536]{1,0:T(8,128)} %param.10) | copy-start | bytes 294916
  46.7 18.4 %collective-permute-start.3 = (f32[16,1536]{1,0:T(8,128)S(1)}, f32[16,1536]{1,0:T(8,128)S(1)}, u32[]{:S(2)}, u32[]{:S(2)}) collective-permute-start(f32[16,1536]{1,0:T(8,128)S(1)} %get-tuple-element.18), channel_id=1, source_target_pairs={{0,1022},{1,1023},{2,0},{3,1},{4,2},{5,3},{6,4},{7,5},{8,6},{9,7},... | collective-permute-start | bytes 294920 | tf_op jit(solution)/shard_map/ppermute | solution.py:171
  61.3 3.8 %copy-start.3 = (f32[1536]{0:T(1024)S(1)}, f32[1536]{0:T(1024)}, u32[]{:S(2)}) copy-start(f32[1536]{0:T(1024)} %param.8) | copy-start | bytes 18436
  65.3 29.1 %copy-start.2 = (f32[16,1536]{1,0:T(8,128)S(1)}, f32[16,1536]{1,0:T(8,128)}, u32[]{:S(2)}) copy-start(f32[16,1536]{1,0:T(8,128)} %param.9) | copy-start | bytes 294916

commit v6 on v5

--- a/solution.py
+++ b/solution.py
@@ -183,16 +183,16 @@
     rhs = direction.shape[0]
     packed = jnp.concatenate([coords, direction], axis=0)
     inv = inv_scale[:, None]
+    left2 = shifted(packed, 2)
     right = shifted(packed, -1)
-    left2 = shifted(packed, 2)
     left, sides = prepare(packed, inv)
-    near_right, to_right = own_pair(left, sides, right, inv)
-    to_left2, to_right = far_pair(left2, right, inv, to_right)
+    near_left2, to_left2 = own_pair(left, sides, left2, inv)
+    to_right, to_left2 = far_pair(right, left2, inv, to_left2)
+    from_right2 = shifted(to_left2, -2)
+    near_right, to_right = own_pair(left, sides, right, inv, to_right)
     from_left = shifted(to_right, 1)
-    near_left2, to_left2 = own_pair(left, sides, left2, inv, to_left2)
-    from_right2 = shifted(to_left2, -2)
-    own = own_block(left, sides, packed, inv, from_left)
-    gp_image = noise_var[None, :] * direction + near_right + near_left2 + own + from_right2
+    own = own_block(left, sides, packed, inv, from_right2)
+    gp_image = noise_var[None, :] * direction + near_right + near_left2 + own + from_left
     sums = [
         jnp.sum(residual * residual, axis=1),
         jnp.sum(direction * gp_image, axis=1),

time: 95.6 us -> 91.3 us (0.955)
  starting transfers between devices: 36.7 us -> 25 us
  waiting for transfers between devices: 4.71 us -> 9.1 us
  blocking collectives: 28.9 us -> 31.9 us
    ppermute x4, starting transfers between devices: 36.7 us -> 25 us  [shifted(): return lax.ppermute(value, AXES, pairs)]
    ppermute x4, waiting for transfers between devices: 4.71 us -> 9.1 us  [shifted(): return lax.ppermute(value, AXES, pairs)]
    all_to_all x2, blocking collectives: 28.9 us -> 31.9 us  [total(): values = jnp.sum(lax.all_to_all(copies, axis, 0, 0, tiled=True), axis=0)]
where the time goes in v6:
time: 91.3 us; the launch traced here: 90.9 us
  blocking collectives  31.9 us (35%)
  starting transfers between devices  25 us (27%)
  Pallas kernels  22 us (24%)
  waiting for transfers between devices  9.1 us (10%)
  other arithmetic  1.2 us (1%)
  local copies, waits for them, and re-layouts  1.06 us (1%)
    all_to_all x2, blocking collectives, total(): values = jnp.sum(lax.all_to_all(copies, axis, 0, 0, tiled=True), axis=0)  31.9 us
    ppermute x4, starting transfers between devices, shifted(): return lax.ppermute(value, AXES, pairs)  25 us
    pallas_call x2, Pallas kernels, own_pair(): call(own_pair_body, 'own_pair', (out, out), 6 * 10 ** 9)  11.9 us
    ppermute x4, waiting for transfers between devices, shifted(): return lax.ppermute(value, AXES, pairs)  9.1 us
    pallas_call x1, Pallas kernels, far_pair(): call(far_pair_body, 'far_pair', (out, out), 6 * 10 ** 9)  6.13 us
    pallas_call x1, Pallas kernels, own_block(): call(self_body, 'own', shape(16, packed.shape[1]), 4 * 10 ** 9)  3.75 us
  transfers between devices with their start and end apart: 4, of which 1 were waited for; matrix products, arithmetic and copies ran while one was open for 0% of the time, Pallas kernels for 17%

profile of v6, /device:TPU:1, one launch (start us, length us, event | category | flops | bytes accessed | tf_op | source)
XLA Modules:
  0.0 90.9 jit_solution(9214122137842408913)
XLA Ops:
  0.6 0.0 copy-start
  0.6 0.8 constant_dynamic-update-slice_fusion.1
  1.5 0.1 copy-done
  1.6 0.0 copy-start.4
  1.6 4.8 %collective-permute-start.1 = (f32[24,1536]{1,0:T(8,128)S(1)}, f32[24,1536]{1,0:T(8,128)S(1)}, u32[]{:S(2)}, u32[]{:S(2)}) collective-permute-start(f32[24,1536]{1,0:T(8,128)S(1)} %constant_dynamic-update-slice_fusion.packed_ref.own_ref), channel_id=1, source_target_pairs={{0,2},{1,3},{2,4},{3,5},{4,6},{5,7},{6,8},{7,9},{8,10},{9,11},{10,... | collective-permute-start | bytes 442376 | tf_op jit(solution)/shard_map/ppermute | solution.py:171
  6.4 13.2 %collective-permute-start = (f32[24,1536]{1,0:T(8,128)S(1)}, f32[24,1536]{1,0:T(8,128)S(1)}, u32[]{:S(2)}, u32[]{:S(2)}) collective-permute-start(f32[24,1536]{1,0:T(8,128)S(1)} %constant_dynamic-update-slice_fusion.packed_ref.own_ref), channel_id=1, source_target_pairs={{0,1023},{1,0},{2,1},{3,2},{4,3},{5,4},{6,5},{7,6},{8,7},{9,8},{10... | collective-permute-start | bytes 442376 | tf_op jit(solution)/shard_map/ppermute | solution.py:171
  19.6 0.0 copy-done.4
  19.6 0.1 copy.19.inv_ref
  19.7 0.2 prepare.1
  19.9 9.1 %collective-permute-done.1.far_ref.other_ref = f32[24,1536]{1,0:T(8,128)S(1)} collective-permute-done((f32[24,1536]{1,0:T(8,128)S(1)}, f32[24,1536]{1,0:T(8,128)S(1)}, u32[]{:S(2)}, u32[]{:S(2)}) %collective-permute-start.1) | collective-permute-done | bytes 147488 | tf_op jit(solution)/shard_map/ppermute | solution.py:171
  29.0 5.9 %own_pair.2 = (f32[16,1536]{1,0:T(8,128)S(1)}, f32[16,1536]{1,0:T(8,128)S(1)}) custom-call(bf16[1536,64]{1,0:T(8,128)(2,1)S(1)} %get-tuple-element.11.left_ref, bf16[32,1536]{1,0:T(8,128)(2,1)S(1)} %get-tuple-element.12.sides_ref, f32[24,1536]{1,0:T(8,128)S(1)} %collective-permute-done.1.far_ref.other_ref, f32[8,1]{1,0:T(8,128)S(1)} %copy.19.inv_ref), custom_call_target="tpu_custom_call" | custom-call | flops 6000000000 | bytes 600000 | tf_op jit(solution)/shard_map/own_pair/pallas_call | solution.py:156
  34.9 0.0 collective-permute-done.one_ref.far_ref
  34.9 6.1 %far_pair.1 = (f32[16,1536]{1,0:T(8,128)S(1)}, f32[16,1536]{1,0:T(8,128)S(1)}) custom-call(f32[24,1536]{1,0:T(8,128)S(1)} %collective-permute-done.one_ref.far_ref, f32[24,1536]{1,0:T(8,128)S(1)} %collective-permute-done.1.far_ref.other_ref, f32[8,1]{1,0:T(8,128)S(1)} %copy.19.inv_ref, f32[16,1536]{1,0:T(8,128)S(1)} %get-tuple-element.13.base_ref), custom_call_target="tpu_custom_call" | custom-call | flops 6000000000 | bytes 600000 | tf_op jit(solution)/shard_map/far_pair/pallas_call | solution.py:161
  41.1 4.5 %collective-permute-start.2 = (f32[16,1536]{1,0:T(8,128)S(1)}, f32[16,1536]{1,0:T(8,128)S(1)}, u32[]{:S(2)}, u32[]{:S(2)}) collective-permute-start(f32[16,1536]{1,0:T(8,128)S(1)} %get-tuple-element.17), channel_id=1, source_target_pairs={{0,1022},{1,1023},{2,0},{3,1},{4,2},{5,3},{6,4},{7,5},{8,6},{9,7},... | collective-permute-start | bytes 294920 | tf_op jit(solution)/shard_map/ppermute | solution.py:171
  45.6 5.9 %own_pair.3 = (f32[16,1536]{1,0:T(8,128)S(1)}, f32[16,1536]{1,0:T(8,128)S(1)}) custom-call(bf16[1536,64]{1,0:T(8,128)(2,1)S(1)} %get-tuple-element.11.left_ref, bf16[32,1536]{1,0:T(8,128)(2,1)S(1)} %get-tuple-element.12.sides_ref, f32[24,1536]{1,0:T(8,128)S(1)} %collective-permute-done.one_ref.far_ref, f32[8,1]{1,0:T(8,128)S(1)} %copy.19.inv_ref, ...), custom_call_target="tpu_custom_call" | custom-call | flops 6000000000 | bytes 600000 | tf_op jit(solution)/shard_map/own_pair/pallas_call | solution.py:156
  51.5 0.0 copy-start.1
  51.5 2.5 %collective-permute-start.3 = (f32[16,1536]{1,0:T(8,128)S(1)}, f32[16,1536]{1,0:T(8,128)S(1)}, u32[]{:S(2)}, u32[]{:S(2)}) collective-permute-start(f32[16,1536]{1,0:T(8,128)S(1)} %get-tuple-element.18), channel_id=1, source_target_pairs={{0,1},{1,2},{2,3},{3,4},{4,5},{5,6},{6,7},{7,8},{8,9},{9,10},{10,1... | collective-permute-start | bytes 294920 | tf_op jit(solution)/shard_map/ppermute | solution.py:171
  54.0 0.0 collective-permute-done.2.base_ref
  54.0 0.0 copy-start.3
  54.1 3.7 %own.1 = f32[16,1536]{1,0:T(8,128)S(1)} custom-call(bf16[1536,64]{1,0:T(8,128)(2,1)S(1)} %get-tuple-element.11.left_ref, bf16[32,1536]{1,0:T(8,128)(2,1)S(1)} %get-tuple-element.12.sides_ref, f32[24,1536]{1,0:T(8,128)S(1)} %constant_dynamic-update-slice_fusion.packed_ref.own_ref, f32[8,1]{1,0:T(8,128)S(1)} %copy.19.inv_ref, ...), custom_call_target="tpu_custom_call" | custom-call | flops 4000000000 | bytes 600000 | tf_op jit(solution)/shard_map/own/pallas_call | solution.py:165
  57.8 0.0 collective-permute-done.3
  57.8 0.0 copy-done.1
  57.8 0.0 copy-done.3
  57.8 0.2 multiply_reduce_fusion.3
  58.0 0.0 copy-start.2
  58.0 0.1 pad_maximum_fusion
  58.1 20.3 %all_to_all.12 = f32[32,1,64]{2,1,0:T(1,128)S(1)} all-to-all(f32[32,1,64]{2,1,0:T(1,128)S(1)} %broadcast_in_dim.7), channel_id=1, replica_groups=mesh['hi'=32,'lo'=32] {'lo'}, dimensions={0} | all-to-all | bytes 16384 | tf_op jit(solution)/shard_map/all_to_all | solution.py:178
  78.4 11.6 %all_to_all.13 = f32[32,1,64]{2,1,0:T(1,128)S(1)} all-to-all(f32[32,1,64]{2,1,0:T(1,128)S(1)} %broadcast_in_dim.8), channel_id=1, replica_groups=mesh['hi'=32,'lo'=32] {'hi'}, dimensions={0} | all-to-all | bytes 16384 | tf_op jit(solution)/shard_map/all_to_all | solution.py:178
  90.0 0.1 maximum_divide_fusion
  90.1 0.0 copy-done.2
  90.1 0.8 multiply_add_fusion
  (5 shorter events, 0.1 us)
Async XLA Ops:
  0.6 0.9 %copy-start = (f32[16,1536]{1,0:T(8,128)S(1)}, f32[16,1536]{1,0:T(8,128)}, u32[]{:S(2)}) copy-start(f32[16,1536]{1,0:T(8,128)} %param.11) | copy-start | bytes 294916
  1.6 18.0 %copy-start.4 = (f32[8]{0:T(128)S(1)}, f32[8]{0:T(128)}, u32[]{:S(2)}) copy-start(f32[8]{0:T(128)} %param.7) | copy-start | bytes 100
  1.6 27.4 %collective-permute-start.1 = (f32[24,1536]{1,0:T(8,128)S(1)}, f32[24,1536]{1,0:T(8,128)S(1)}, u32[]{:S(2)}, u32[]{:S(2)}) collective-permute-start(f32[24,1536]{1,0:T(8,128)S(1)} %constant_dynamic-update-slice_fusion.packed_ref.own_ref), channel_id=1, source_target_pairs={{0,2},{1,3},{2,4},{3,5},{4,6},{5,7},{6,8},{7,9},{8,10},{9,11},{10,... | collective-permute-start | bytes 442376 | tf_op jit(solution)/shard_map/ppermute | solution.py:171
  6.4 28.5 %collective-permute-start = (f32[24,1536]{1,0:T(8,128)S(1)}, f32[24,1536]{1,0:T(8,128)S(1)}, u32[]{:S(2)}, u32[]{:S(2)}) collective-permute-start(f32[24,1536]{1,0:T(8,128)S(1)} %constant_dynamic-update-slice_fusion.packed_ref.own_ref), channel_id=1, source_target_pairs={{0,1023},{1,0},{2,1},{3,2},{4,3},{5,4},{6,5},{7,6},{8,7},{9,8},{10... | collective-permute-start | bytes 442376 | tf_op jit(solution)/shard_map/ppermute | solution.py:171
  41.1 13.0 %collective-permute-start.2 = (f32[16,1536]{1,0:T(8,128)S(1)}, f32[16,1536]{1,0:T(8,128)S(1)}, u32[]{:S(2)}, u32[]{:S(2)}) collective-permute-start(f32[16,1536]{1,0:T(8,128)S(1)} %get-tuple-element.17), channel_id=1, source_target_pairs={{0,1022},{1,1023},{2,0},{3,1},{4,2},{5,3},{6,4},{7,5},{8,6},{9,7},... | collective-permute-start | bytes 294920 | tf_op jit(solution)/shard_map/ppermute | solution.py:171
  51.5 6.3 %copy-start.1 = (f32[16,1536]{1,0:T(8,128)S(1)}, f32[16,1536]{1,0:T(8,128)}, u32[]{:S(2)}) copy-start(f32[16,1536]{1,0:T(8,128)} %param.10) | copy-start | bytes 294916
  51.5 6.3 %collective-permute-start.3 = (f32[16,1536]{1,0:T(8,128)S(1)}, f32[16,1536]{1,0:T(8,128)S(1)}, u32[]{:S(2)}, u32[]{:S(2)}) collective-permute-start(f32[16,1536]{1,0:T(8,128)S(1)} %get-tuple-element.18), channel_id=1, source_target_pairs={{0,1},{1,2},{2,3},{3,4},{4,5},{5,6},{6,7},{7,8},{8,9},{9,10},{10,1... | collective-permute-start | bytes 294920 | tf_op jit(solution)/shard_map/ppermute | solution.py:171
  54.0 3.8 %copy-start.3 = (f32[1536]{0:T(1024)S(1)}, f32[1536]{0:T(1024)}, u32[]{:S(2)}) copy-start(f32[1536]{0:T(1024)} %param.8) | copy-start | bytes 18436
  58.0 32.1 %copy-start.2 = (f32[16,1536]{1,0:T(8,128)S(1)}, f32[16,1536]{1,0:T(8,128)}, u32[]{:S(2)}) copy-start(f32[16,1536]{1,0:T(8,128)} %param.9) | copy-start | bytes 294916

commit v7 on v6

--- a/solution.py
+++ b/solution.py
@@ -59,8 +59,8 @@
 
 def covariance(squared):
     squared = jnp.maximum(squared, TINY)
-    dist = squared * lax.rsqrt(squared)
-    return ((dist + LINEAR) * dist + CONSTANT) * jnp.exp2(-dist)
+    less = -squared * lax.rsqrt(squared)
+    return ((squared + CONSTANT) - LINEAR * less) * jnp.exp2(less)
 
 
 def product(left, right):

time: 91.3 us -> 90.1 us (0.987)
  Pallas kernels: 22 us -> 20.5 us
where the time goes in v7:
time: 90.1 us; the launch traced here: 89.7 us
  blocking collectives  32.1 us (36%)
  starting transfers between devices  25 us (28%)
  Pallas kernels  20.5 us (23%)
  waiting for transfers between devices  9.1 us (10%)
  other arithmetic  1.2 us (1%)
  local copies, waits for them, and re-layouts  1.06 us (1%)
    all_to_all x2, blocking collectives, total(): values = jnp.sum(lax.all_to_all(copies, axis, 0, 0, tiled=True), axis=0)  32.1 us
    ppermute x4, starting transfers between devices, shifted(): return lax.ppermute(value, AXES, pairs)  25 us
    pallas_call x2, Pallas kernels, own_pair(): call(own_pair_body, 'own_pair', (out, out), 6 * 10 ** 9)  11 us
    ppermute x4, waiting for transfers between devices, shifted(): return lax.ppermute(value, AXES, pairs)  9.1 us
    pallas_call x1, Pallas kernels, far_pair(): call(far_pair_body, 'far_pair', (out, out), 6 * 10 ** 9)  5.71 us
    pallas_call x1, Pallas kernels, own_block(): call(self_body, 'own', shape(16, packed.shape[1]), 4 * 10 ** 9)  3.52 us
  transfers between devices with their start and end apart: 4, of which 1 were waited for; matrix products, arithmetic and copies ran while one was open for 0% of the time, Pallas kernels for 17%

profile of v7, /device:TPU:1, one launch (start us, length us, event | category | flops | bytes accessed | tf_op | source)
XLA Modules:
  0.0 89.7 jit_solution(1763298115033262002)
XLA Ops:
  0.6 0.0 copy-start
  0.6 0.8 constant_dynamic-update-slice_fusion.1
  1.5 0.1 copy-done
  1.6 0.0 copy-start.4
  1.6 4.8 %collective-permute-start.1 = (f32[24,1536]{1,0:T(8,128)S(1)}, f32[24,1536]{1,0:T(8,128)S(1)}, u32[]{:S(2)}, u32[]{:S(2)}) collective-permute-start(f32[24,1536]{1,0:T(8,128)S(1)} %constant_dynamic-update-slice_fusion.packed_ref.own_ref), channel_id=1, source_target_pairs={{0,2},{1,3},{2,4},{3,5},{4,6},{5,7},{6,8},{7,9},{8,10},{9,11},{10,... | collective-permute-start | bytes 442376 | tf_op jit(solution)/shard_map/ppermute | solution.py:171
  6.4 13.2 %collective-permute-start = (f32[24,1536]{1,0:T(8,128)S(1)}, f32[24,1536]{1,0:T(8,128)S(1)}, u32[]{:S(2)}, u32[]{:S(2)}) collective-permute-start(f32[24,1536]{1,0:T(8,128)S(1)} %constant_dynamic-update-slice_fusion.packed_ref.own_ref), channel_id=1, source_target_pairs={{0,1023},{1,0},{2,1},{3,2},{4,3},{5,4},{6,5},{7,6},{8,7},{9,8},{10... | collective-permute-start | bytes 442376 | tf_op jit(solution)/shard_map/ppermute | solution.py:171
  19.6 0.0 copy-done.4
  19.6 0.1 copy.19.inv_ref
  19.7 0.2 prepare.1
  19.9 9.1 %collective-permute-done.1.far_ref.other_ref = f32[24,1536]{1,0:T(8,128)S(1)} collective-permute-done((f32[24,1536]{1,0:T(8,128)S(1)}, f32[24,1536]{1,0:T(8,128)S(1)}, u32[]{:S(2)}, u32[]{:S(2)}) %collective-permute-start.1) | collective-permute-done | bytes 147488 | tf_op jit(solution)/shard_map/ppermute | solution.py:171
  29.0 5.5 %own_pair.2 = (f32[16,1536]{1,0:T(8,128)S(1)}, f32[16,1536]{1,0:T(8,128)S(1)}) custom-call(bf16[1536,64]{1,0:T(8,128)(2,1)S(1)} %get-tuple-element.11.left_ref, bf16[32,1536]{1,0:T(8,128)(2,1)S(1)} %get-tuple-element.12.sides_ref, f32[24,1536]{1,0:T(8,128)S(1)} %collective-permute-done.1.far_ref.other_ref, f32[8,1]{1,0:T(8,128)S(1)} %copy.19.inv_ref), custom_call_target="tpu_custom_call" | custom-call | flops 6000000000 | bytes 600000 | tf_op jit(solution)/shard_map/own_pair/pallas_call | solution.py:156
  34.5 0.0 collective-permute-done.one_ref.far_ref
  34.5 5.7 %far_pair.1 = (f32[16,1536]{1,0:T(8,128)S(1)}, f32[16,1536]{1,0:T(8,128)S(1)}) custom-call(f32[24,1536]{1,0:T(8,128)S(1)} %collective-permute-done.one_ref.far_ref, f32[24,1536]{1,0:T(8,128)S(1)} %collective-permute-done.1.far_ref.other_ref, f32[8,1]{1,0:T(8,128)S(1)} %copy.19.inv_ref, f32[16,1536]{1,0:T(8,128)S(1)} %get-tuple-element.13.base_ref), custom_call_target="tpu_custom_call" | custom-call | flops 6000000000 | bytes 600000 | tf_op jit(solution)/shard_map/far_pair/pallas_call | solution.py:161
  40.2 4.9 %collective-permute-start.2 = (f32[16,1536]{1,0:T(8,128)S(1)}, f32[16,1536]{1,0:T(8,128)S(1)}, u32[]{:S(2)}, u32[]{:S(2)}) collective-permute-start(f32[16,1536]{1,0:T(8,128)S(1)} %get-tuple-element.17), channel_id=1, source_target_pairs={{0,1022},{1,1023},{2,0},{3,1},{4,2},{5,3},{6,4},{7,5},{8,6},{9,7},... | collective-permute-start | bytes 294920 | tf_op jit(solution)/shard_map/ppermute | solution.py:171
  45.1 5.5 %own_pair.3 = (f32[16,1536]{1,0:T(8,128)S(1)}, f32[16,1536]{1,0:T(8,128)S(1)}) custom-call(bf16[1536,64]{1,0:T(8,128)(2,1)S(1)} %get-tuple-element.11.left_ref, bf16[32,1536]{1,0:T(8,128)(2,1)S(1)} %get-tuple-element.12.sides_ref, f32[24,1536]{1,0:T(8,128)S(1)} %collective-permute-done.one_ref.far_ref, f32[8,1]{1,0:T(8,128)S(1)} %copy.19.inv_ref, ...), custom_call_target="tpu_custom_call" | custom-call | flops 6000000000 | bytes 600000 | tf_op jit(solution)/shard_map/own_pair/pallas_call | solution.py:156
  50.7 0.0 copy-start.1
  50.7 2.1 %collective-permute-start.3 = (f32[16,1536]{1,0:T(8,128)S(1)}, f32[16,1536]{1,0:T(8,128)S(1)}, u32[]{:S(2)}, u32[]{:S(2)}) collective-permute-start(f32[16,1536]{1,0:T(8,128)S(1)} %get-tuple-element.18), channel_id=1, source_target_pairs={{0,1},{1,2},{2,3},{3,4},{4,5},{5,6},{6,7},{7,8},{8,9},{9,10},{10,1... | collective-permute-start | bytes 294920 | tf_op jit(solution)/shard_map/ppermute | solution.py:171
  52.8 0.0 collective-permute-done.2.base_ref
  52.8 0.0 copy-start.3
  52.8 3.5 %own.1 = f32[16,1536]{1,0:T(8,128)S(1)} custom-call(bf16[1536,64]{1,0:T(8,128)(2,1)S(1)} %get-tuple-element.11.left_ref, bf16[32,1536]{1,0:T(8,128)(2,1)S(1)} %get-tuple-element.12.sides_ref, f32[24,1536]{1,0:T(8,128)S(1)} %constant_dynamic-update-slice_fusion.packed_ref.own_ref, f32[8,1]{1,0:T(8,128)S(1)} %copy.19.inv_ref, ...), custom_call_target="tpu_custom_call" | custom-call | flops 4000000000 | bytes 600000 | tf_op jit(solution)/shard_map/own/pallas_call | solution.py:165
  56.3 0.0 collective-permute-done.3
  56.3 0.0 copy-done.1
  56.4 0.0 copy-done.3
  56.4 0.2 multiply_reduce_fusion.3
  56.6 0.0 copy-start.2
  56.6 0.1 pad_maximum_fusion
  56.7 20.5 %all_to_all.12 = f32[32,1,64]{2,1,0:T(1,128)S(1)} all-to-all(f32[32,1,64]{2,1,0:T(1,128)S(1)} %broadcast_in_dim.7), channel_id=1, replica_groups=mesh['hi'=32,'lo'=32] {'lo'}, dimensions={0} | all-to-all | bytes 16384 | tf_op jit(solution)/shard_map/all_to_all | solution.py:178
  77.2 11.6 %all_to_all.13 = f32[32,1,64]{2,1,0:T(1,128)S(1)} all-to-all(f32[32,1,64]{2,1,0:T(1,128)S(1)} %broadcast_in_dim.8), channel_id=1, replica_groups=mesh['hi'=32,'lo'=32] {'hi'}, dimensions={0} | all-to-all | bytes 16384 | tf_op jit(solution)/shard_map/all_to_all | solution.py:178
  88.8 0.1 maximum_divide_fusion
  88.9 0.0 copy-done.2
  88.9 0.8 multiply_add_fusion
  (5 shorter events, 0.1 us)
Async XLA Ops:
  0.6 0.9 %copy-start = (f32[16,1536]{1,0:T(8,128)S(1)}, f32[16,1536]{1,0:T(8,128)}, u32[]{:S(2)}) copy-start(f32[16,1536]{1,0:T(8,128)} %param.11) | copy-start | bytes 294916
  1.6 18.0 %copy-start.4 = (f32[8]{0:T(128)S(1)}, f32[8]{0:T(128)}, u32[]{:S(2)}) copy-start(f32[8]{0:T(128)} %param.7) | copy-start | bytes 100
  1.6 27.4 %collective-permute-start.1 = (f32[24,1536]{1,0:T(8,128)S(1)}, f32[24,1536]{1,0:T(8,128)S(1)}, u32[]{:S(2)}, u32[]{:S(2)}) collective-permute-start(f32[24,1536]{1,0:T(8,128)S(1)} %constant_dynamic-update-slice_fusion.packed_ref.own_ref), channel_id=1, source_target_pairs={{0,2},{1,3},{2,4},{3,5},{4,6},{5,7},{6,8},{7,9},{8,10},{9,11},{10,... | collective-permute-start | bytes 442376 | tf_op jit(solution)/shard_map/ppermute | solution.py:171
  6.4 28.1 %collective-permute-start = (f32[24,1536]{1,0:T(8,128)S(1)}, f32[24,1536]{1,0:T(8,128)S(1)}, u32[]{:S(2)}, u32[]{:S(2)}) collective-permute-start(f32[24,1536]{1,0:T(8,128)S(1)} %constant_dynamic-update-slice_fusion.packed_ref.own_ref), channel_id=1, source_target_pairs={{0,1023},{1,0},{2,1},{3,2},{4,3},{5,4},{6,5},{7,6},{8,7},{9,8},{10... | collective-permute-start | bytes 442376 | tf_op jit(solution)/shard_map/ppermute | solution.py:171
  40.2 12.6 %collective-permute-start.2 = (f32[16,1536]{1,0:T(8,128)S(1)}, f32[16,1536]{1,0:T(8,128)S(1)}, u32[]{:S(2)}, u32[]{:S(2)}) collective-permute-start(f32[16,1536]{1,0:T(8,128)S(1)} %get-tuple-element.17), channel_id=1, source_target_pairs={{0,1022},{1,1023},{2,0},{3,1},{4,2},{5,3},{6,4},{7,5},{8,6},{9,7},... | collective-permute-start | bytes 294920 | tf_op jit(solution)/shard_map/ppermute | solution.py:171
  50.7 5.7 %copy-start.1 = (f32[16,1536]{1,0:T(8,128)S(1)}, f32[16,1536]{1,0:T(8,128)}, u32[]{:S(2)}) copy-start(f32[16,1536]{1,0:T(8,128)} %param.10) | copy-start | bytes 294916
  50.7 5.7 %collective-permute-start.3 = (f32[16,1536]{1,0:T(8,128)S(1)}, f32[16,1536]{1,0:T(8,128)S(1)}, u32[]{:S(2)}, u32[]{:S(2)}) collective-permute-start(f32[16,1536]{1,0:T(8,128)S(1)} %get-tuple-element.18), channel_id=1, source_target_pairs={{0,1},{1,2},{2,3},{3,4},{4,5},{5,6},{6,7},{7,8},{8,9},{9,10},{10,1... | collective-permute-start | bytes 294920 | tf_op jit(solution)/shard_map/ppermute | solution.py:171
  52.8 3.6 %copy-start.3 = (f32[1536]{0:T(1024)S(1)}, f32[1536]{0:T(1024)}, u32[]{:S(2)}) copy-start(f32[1536]{0:T(1024)} %param.8) | copy-start | bytes 18436
  56.6 32.3 %copy-start.2 = (f32[16,1536]{1,0:T(8,128)S(1)}, f32[16,1536]{1,0:T(8,128)}, u32[]{:S(2)}) copy-start(f32[16,1536]{1,0:T(8,128)} %param.9) | copy-start | bytes 294916

commit v8 on v7

--- a/solution.py
+++ b/solution.py
@@ -106,9 +106,13 @@
     near_ref[...] = near
 
 
-def own_pair_body(left_ref, sides_ref, far_ref, inv_ref, *refs):
-    base_ref = refs[0] if len(refs) == 3 else None
-    block_products(left_ref[...], sides_ref[...], far_ref, inv_ref, base_ref, refs[-2], refs[-1])
+def own_pair_body(left_ref, sides_ref, far_ref, inv_ref, base_ref, near_ref, back_ref):
+    block_products(left_ref[...], sides_ref[...], far_ref, inv_ref, base_ref, near_ref, back_ref)
+
+
+def first_pair_body(left_ref, sides_ref, far_ref, inv_ref, near_base_ref, near_ref, back_ref):
+    block_products(left_ref[...], sides_ref[...], far_ref, inv_ref, None, near_ref, back_ref)
+    near_ref[...] += near_base_ref[...]
 
 
 def far_pair_body(one_ref, other_ref, inv_ref, base_ref, near_ref, back_ref):
@@ -116,19 +120,20 @@
     block_products(left, sides, other_ref, inv_ref, base_ref, near_ref, back_ref)
 
 
-def self_body(left_ref, sides_ref, own_ref, inv_ref, base_ref, out_ref):
-    sites = own_ref.shape[1]
+def self_body(tiles, left_ref, sides_ref, own_ref, inv_ref, *refs):
+    out_ref = refs[-1]
     right, _ = right_side(own_ref, inv_ref)
     out_ref[...] = jnp.zeros_like(out_ref)
-    for start in range(0, sites, TILE):
-        stop = start + TILE
+    for tile in tiles:
+        start, stop = tile * TILE, (tile + 1) * TILE
         columns = slice(start, stop)
         values = covariance(product(left_ref[0:stop, :], right[:, columns]))
         high, low = split2(values)
         out_ref[:, 0:stop] += applied(product_t, sides_ref[:, columns], high, low)
         if start:
             out_ref[:, columns] += applied(product, sides_ref[:, 0:start], high[0:start], low[0:start])
-    out_ref[...] = (2.0 * ROUNDS) * out_ref[...] + base_ref[...]
+    out = (2.0 * ROUNDS) * out_ref[...]
+    out_ref[...] = out + refs[0][...] if len(refs) == 2 else out
 
 
 def call(body, name, shapes, cost):
@@ -151,9 +156,14 @@
     return call(prepare_body, "prepare", shapes, 10**7)(packed, inv)
 
 
-def own_pair(left, sides, far, inv, *base):
+def own_pair(left, sides, far, inv, base):
     out = shape(16, far.shape[1])
-    return call(own_pair_body, "own_pair", (out, out), 6 * 10**9)(left, sides, far, inv, *base)
+    return call(own_pair_body, "own_pair", (out, out), 6 * 10**9)(left, sides, far, inv, base)
+
+
+def first_pair(left, sides, far, inv, near_base):
+    out = shape(16, far.shape[1])
+    return call(first_pair_body, "first_pair", (out, out), 6 * 10**9)(left, sides, far, inv, near_base)
 
 
 def far_pair(one, other, inv, base):
@@ -161,8 +171,9 @@
     return call(far_pair_body, "far_pair", (out, out), 6 * 10**9)(one, other, inv, base)
 
 
-def own_block(left, sides, packed, inv, base):
-    return call(self_body, "own", shape(16, packed.shape[1]), 4 * 10**9)(left, sides, packed, inv, base)
+def own_block(tiles, left, sides, packed, inv, *base):
+    body = functools.partial(self_body, tiles)
+    return call(body, "own", shape(16, packed.shape[1]), 2 * 10**9)(left, sides, packed, inv, *base)
 
 
 def shifted(value, steps):
@@ -186,12 +197,15 @@
     left2 = shifted(packed, 2)
     right = shifted(packed, -1)
     left, sides = prepare(packed, inv)
-    near_left2, to_left2 = own_pair(left, sides, left2, inv)
+    count = packed.shape[1] // TILE
+    early = count - count // 3
+    own_early = own_block(range(early), left, sides, packed, inv)
+    near_left2, to_left2 = first_pair(left, sides, left2, inv, own_early)
     to_right, to_left2 = far_pair(right, left2, inv, to_left2)
     from_right2 = shifted(to_left2, -2)
     near_right, to_right = own_pair(left, sides, right, inv, to_right)
     from_left = shifted(to_right, 1)
-    own = own_block(left, sides, packed, inv, from_right2)
+    own = own_block(range(early, count), left, sides, packed, inv, from_right2)
     gp_image = noise_var[None, :] * direction + near_right + near_left2 + own + from_left
     sums = [
         jnp.sum(residual * residual, axis=1),

time: 90.1 us -> 90.1 us (level)
  waiting for transfers between devices: 9.1 us -> 7.19 us
  blocking collectives: 32.1 us -> 33.5 us
    pallas_call x1 -> x3, Pallas kernels: 3.52 us -> 9.55 us  [the longest x1 5.52 us: first_pair(): call(first_pair_body, 'first_pair', (out, out), 6 * 10 ** 9)]
    pallas_call x2 -> x1, Pallas kernels: 11 us -> 5.52 us  [own_pair(): call(own_pair_body, 'own_pair', (out, out), 6 * 10 ** 9)]
    ppermute x4, waiting for transfers between devices: 9.1 us -> 7.19 us  [shifted(): return lax.ppermute(value, AXES, pairs)]
    all_to_all x2, blocking collectives: 32.1 us -> 33.5 us  [total(): values = jnp.sum(lax.all_to_all(copies, axis, 0, 0, tiled=True), axis=0)]
where the time goes in v8:
time: 90.1 us; the launch traced here: 89.7 us
  blocking collectives  33.5 us (37%)
  starting transfers between devices  25 us (28%)
  Pallas kernels  21 us (23%)
  waiting for transfers between devices  7.19 us (8%)
  other arithmetic  1.2 us (1%)
  local copies, waits for them, and re-layouts  1.06 us (1%)
    all_to_all x2, blocking collectives, total(): values = jnp.sum(lax.all_to_all(copies, axis, 0, 0, tiled=True), axis=0)  33.5 us
    ppermute x4, starting transfers between devices, shifted(): return lax.ppermute(value, AXES, pairs)  25 us
    ppermute x4, waiting for transfers between devices, shifted(): return lax.ppermute(value, AXES, pairs)  7.19 us
    pallas_call x1, Pallas kernels, far_pair(): call(far_pair_body, 'far_pair', (out, out), 6 * 10 ** 9)  5.71 us
    pallas_call x1, Pallas kernels, own_pair(): call(own_pair_body, 'own_pair', (out, out), 6 * 10 ** 9)  5.52 us
    pallas_call x1, Pallas kernels, first_pair(): call(first_pair_body, 'first_pair', (out, out), 6 * 10 ** 9)  5.52 us
    pallas_call x2, Pallas kernels, own_block(): call(body, 'own', shape(16, packed.shape[1]), 2 * 10 ** 9)  4.03 us
  transfers between devices with their start and end apart: 4, of which 1 were waited for; matrix products, arithmetic and copies ran while one was open for 0% of the time, Pallas kernels for 17%

profile of v8, /device:TPU:1, one launch (start us, length us, event | category | flops | bytes accessed | tf_op | source)
XLA Modules:
  0.0 89.7 jit_solution(6374149843323084709)
XLA Ops:
  0.6 0.0 copy-start
  0.6 0.8 constant_dynamic-update-slice_fusion.1
  1.5 0.1 copy-done
  1.6 0.0 copy-start.4
  1.6 4.8 %collective-permute-start.1 = (f32[24,1536]{1,0:T(8,128)S(1)}, f32[24,1536]{1,0:T(8,128)S(1)}, u32[]{:S(2)}, u32[]{:S(2)}) collective-permute-start(f32[24,1536]{1,0:T(8,128)S(1)} %constant_dynamic-update-slice_fusion.packed_ref.own_ref), channel_id=1, source_target_pairs={{0,2},{1,3},{2,4},{3,5},{4,6},{5,7},{6,8},{7,9},{8,10},{9,11},{10,... | collective-permute-start | bytes 442376 | tf_op jit(solution)/shard_map/ppermute | solution.py:182
  6.4 13.2 %collective-permute-start = (f32[24,1536]{1,0:T(8,128)S(1)}, f32[24,1536]{1,0:T(8,128)S(1)}, u32[]{:S(2)}, u32[]{:S(2)}) collective-permute-start(f32[24,1536]{1,0:T(8,128)S(1)} %constant_dynamic-update-slice_fusion.packed_ref.own_ref), channel_id=1, source_target_pairs={{0,1023},{1,0},{2,1},{3,2},{4,3},{5,4},{6,5},{7,6},{8,7},{9,8},{10... | collective-permute-start | bytes 442376 | tf_op jit(solution)/shard_map/ppermute | solution.py:182
  19.6 0.0 copy-done.4
  19.6 0.1 copy.21.inv_ref
  19.7 0.2 prepare.1
  19.9 1.9 %own.2.near_base_ref = f32[16,1536]{1,0:T(8,128)S(1)} custom-call(bf16[1536,64]{1,0:T(8,128)(2,1)S(1)} %get-tuple-element.11.left_ref, bf16[32,1536]{1,0:T(8,128)(2,1)S(1)} %get-tuple-element.12.sides_ref, f32[24,1536]{1,0:T(8,128)S(1)} %constant_dynamic-update-slice_fusion.packed_ref.own_ref, f32[8,1]{1,0:T(8,128)S(1)} %copy.21.inv_ref), custom_call_target="tpu_custom_call" | custom-call | flops 2000000000 | bytes 600000 | tf_op jit(solution)/shard_map/own/pallas_call | solution.py:176
  21.8 7.2 %collective-permute-done.1.far_ref.other_ref = f32[24,1536]{1,0:T(8,128)S(1)} collective-permute-done((f32[24,1536]{1,0:T(8,128)S(1)}, f32[24,1536]{1,0:T(8,128)S(1)}, u32[]{:S(2)}, u32[]{:S(2)}) %collective-permute-start.1) | collective-permute-done | bytes 147488 | tf_op jit(solution)/shard_map/ppermute | solution.py:182
  29.0 5.5 %first_pair.1 = (f32[16,1536]{1,0:T(8,128)S(1)}, f32[16,1536]{1,0:T(8,128)S(1)}) custom-call(bf16[1536,64]{1,0:T(8,128)(2,1)S(1)} %get-tuple-element.11.left_ref, bf16[32,1536]{1,0:T(8,128)(2,1)S(1)} %get-tuple-element.12.sides_ref, f32[24,1536]{1,0:T(8,128)S(1)} %collective-permute-done.1.far_ref.other_ref, f32[8,1]{1,0:T(8,128)S(1)} %copy.21.inv_ref, ...), custom_call_target="tpu_custom_call" | custom-call | flops 6000000000 | bytes 600000 | tf_op jit(solution)/shard_map/first_pair/pallas_call | solution.py:166
  34.5 0.0 collective-permute-done.one_ref.far_ref
  34.5 5.7 %far_pair.1 = (f32[16,1536]{1,0:T(8,128)S(1)}, f32[16,1536]{1,0:T(8,128)S(1)}) custom-call(f32[24,1536]{1,0:T(8,128)S(1)} %collective-permute-done.one_ref.far_ref, f32[24,1536]{1,0:T(8,128)S(1)} %collective-permute-done.1.far_ref.other_ref, f32[8,1]{1,0:T(8,128)S(1)} %copy.21.inv_ref, f32[16,1536]{1,0:T(8,128)S(1)} %get-tuple-element.13.base_ref), custom_call_target="tpu_custom_call" | custom-call | flops 6000000000 | bytes 600000 | tf_op jit(solution)/shard_map/far_pair/pallas_call | solution.py:171
  40.2 4.9 %collective-permute-start.2 = (f32[16,1536]{1,0:T(8,128)S(1)}, f32[16,1536]{1,0:T(8,128)S(1)}, u32[]{:S(2)}, u32[]{:S(2)}) collective-permute-start(f32[16,1536]{1,0:T(8,128)S(1)} %get-tuple-element.17), channel_id=1, source_target_pairs={{0,1022},{1,1023},{2,0},{3,1},{4,2},{5,3},{6,4},{7,5},{8,6},{9,7},... | collective-permute-start | bytes 294920 | tf_op jit(solution)/shard_map/ppermute | solution.py:182
  45.1 5.5 %own_pair.1 = (f32[16,1536]{1,0:T(8,128)S(1)}, f32[16,1536]{1,0:T(8,128)S(1)}) custom-call(bf16[1536,64]{1,0:T(8,128)(2,1)S(1)} %get-tuple-element.11.left_ref, bf16[32,1536]{1,0:T(8,128)(2,1)S(1)} %get-tuple-element.12.sides_ref, f32[24,1536]{1,0:T(8,128)S(1)} %collective-permute-done.one_ref.far_ref, f32[8,1]{1,0:T(8,128)S(1)} %copy.21.inv_ref, ...), custom_call_target="tpu_custom_call" | custom-call | flops 6000000000 | bytes 600000 | tf_op jit(solution)/shard_map/own_pair/pallas_call | solution.py:161
  50.7 0.0 copy-start.1
  50.7 2.1 %collective-permute-start.3 = (f32[16,1536]{1,0:T(8,128)S(1)}, f32[16,1536]{1,0:T(8,128)S(1)}, u32[]{:S(2)}, u32[]{:S(2)}) collective-permute-start(f32[16,1536]{1,0:T(8,128)S(1)} %get-tuple-element.18), channel_id=1, source_target_pairs={{0,1},{1,2},{2,3},{3,4},{4,5},{5,6},{6,7},{7,8},{8,9},{9,10},{10,1... | collective-permute-start | bytes 294920 | tf_op jit(solution)/shard_map/ppermute | solution.py:182
  52.8 0.0 collective-permute-done.2.refs_0_
  52.8 0.0 copy-start.3
  52.8 2.1 %own.3 = f32[16,1536]{1,0:T(8,128)S(1)} custom-call(bf16[1536,64]{1,0:T(8,128)(2,1)S(1)} %get-tuple-element.11.left_ref, bf16[32,1536]{1,0:T(8,128)(2,1)S(1)} %get-tuple-element.12.sides_ref, f32[24,1536]{1,0:T(8,128)S(1)} %constant_dynamic-update-slice_fusion.packed_ref.own_ref, f32[8,1]{1,0:T(8,128)S(1)} %copy.21.inv_ref, ...), custom_call_target="tpu_custom_call" | custom-call | flops 2000000000 | bytes 600000 | tf_op jit(solution)/shard_map/own/pallas_call | solution.py:176
  54.9 0.0 collective-permute-done.3
  54.9 0.0 copy-done.1
  55.0 0.0 copy-done.3
  55.0 0.2 multiply_reduce_fusion.3
  55.2 0.0 copy-start.2
  55.2 0.1 pad_maximum_fusion
  55.3 21.9 %all_to_all.12 = f32[32,1,64]{2,1,0:T(1,128)S(1)} all-to-all(f32[32,1,64]{2,1,0:T(1,128)S(1)} %broadcast_in_dim.7), channel_id=1, replica_groups=mesh['hi'=32,'lo'=32] {'lo'}, dimensions={0} | all-to-all | bytes 16384 | tf_op jit(solution)/shard_map/all_to_all | solution.py:189
  77.2 11.6 %all_to_all.13 = f32[32,1,64]{2,1,0:T(1,128)S(1)} all-to-all(f32[32,1,64]{2,1,0:T(1,128)S(1)} %broadcast_in_dim.8), channel_id=1, replica_groups=mesh['hi'=32,'lo'=32] {'hi'}, dimensions={0} | all-to-all | bytes 16384 | tf_op jit(solution)/shard_map/all_to_all | solution.py:189
  88.8 0.1 maximum_divide_fusion
  88.9 0.0 copy-done.2
  88.9 0.8 multiply_add_fusion
  (5 shorter events, 0.1 us)
Async XLA Ops:
  0.6 0.9 %copy-start = (f32[16,1536]{1,0:T(8,128)S(1)}, f32[16,1536]{1,0:T(8,128)}, u32[]{:S(2)}) copy-start(f32[16,1536]{1,0:T(8,128)} %param.11) | copy-start | bytes 294916
  1.6 18.0 %copy-start.4 = (f32[8]{0:T(128)S(1)}, f32[8]{0:T(128)}, u32[]{:S(2)}) copy-start(f32[8]{0:T(128)} %param.7) | copy-start | bytes 100
  1.6 27.4 %collective-permute-start.1 = (f32[24,1536]{1,0:T(8,128)S(1)}, f32[24,1536]{1,0:T(8,128)S(1)}, u32[]{:S(2)}, u32[]{:S(2)}) collective-permute-start(f32[24,1536]{1,0:T(8,128)S(1)} %constant_dynamic-update-slice_fusion.packed_ref.own_ref), channel_id=1, source_target_pairs={{0,2},{1,3},{2,4},{3,5},{4,6},{5,7},{6,8},{7,9},{8,10},{9,11},{10,... | collective-permute-start | bytes 442376 | tf_op jit(solution)/shard_map/ppermute | solution.py:182
  6.4 28.1 %collective-permute-start = (f32[24,1536]{1,0:T(8,128)S(1)}, f32[24,1536]{1,0:T(8,128)S(1)}, u32[]{:S(2)}, u32[]{:S(2)}) collective-permute-start(f32[24,1536]{1,0:T(8,128)S(1)} %constant_dynamic-update-slice_fusion.packed_ref.own_ref), channel_id=1, source_target_pairs={{0,1023},{1,0},{2,1},{3,2},{4,3},{5,4},{6,5},{7,6},{8,7},{9,8},{10... | collective-permute-start | bytes 442376 | tf_op jit(solution)/shard_map/ppermute | solution.py:182
  40.2 12.6 %collective-permute-start.2 = (f32[16,1536]{1,0:T(8,128)S(1)}, f32[16,1536]{1,0:T(8,128)S(1)}, u32[]{:S(2)}, u32[]{:S(2)}) collective-permute-start(f32[16,1536]{1,0:T(8,128)S(1)} %get-tuple-element.17), channel_id=1, source_target_pairs={{0,1022},{1,1023},{2,0},{3,1},{4,2},{5,3},{6,4},{7,5},{8,6},{9,7},... | collective-permute-start | bytes 294920 | tf_op jit(solution)/shard_map/ppermute | solution.py:182
  50.7 4.3 %copy-start.1 = (f32[16,1536]{1,0:T(8,128)S(1)}, f32[16,1536]{1,0:T(8,128)}, u32[]{:S(2)}) copy-start(f32[16,1536]{1,0:T(8,128)} %param.10) | copy-start | bytes 294916
  50.7 4.3 %collective-permute-start.3 = (f32[16,1536]{1,0:T(8,128)S(1)}, f32[16,1536]{1,0:T(8,128)S(1)}, u32[]{:S(2)}, u32[]{:S(2)}) collective-permute-start(f32[16,1536]{1,0:T(8,128)S(1)} %get-tuple-element.18), channel_id=1, source_target_pairs={{0,1},{1,2},{2,3},{3,4},{4,5},{5,6},{6,7},{7,8},{8,9},{9,10},{10,1... | collective-permute-start | bytes 294920 | tf_op jit(solution)/shard_map/ppermute | solution.py:182
  52.8 2.2 %copy-start.3 = (f32[1536]{0:T(1024)S(1)}, f32[1536]{0:T(1024)}, u32[]{:S(2)}) copy-start(f32[1536]{0:T(1024)} %param.8) | copy-start | bytes 18436
  55.2 33.7 %copy-start.2 = (f32[16,1536]{1,0:T(8,128)S(1)}, f32[16,1536]{1,0:T(8,128)}, u32[]{:S(2)}) copy-start(f32[16,1536]{1,0:T(8,128)} %param.9) | copy-start | bytes 294916

commit v9 on v8

--- a/solution.py
+++ b/solution.py
@@ -198,7 +198,7 @@
     right = shifted(packed, -1)
     left, sides = prepare(packed, inv)
     count = packed.shape[1] // TILE
-    early = count - count // 3
+    early = count // 2
     own_early = own_block(range(early), left, sides, packed, inv)
     near_left2, to_left2 = first_pair(left, sides, left2, inv, own_early)
     to_right, to_left2 = far_pair(right, left2, inv, to_left2)

time: 90.1 us -> 90.1 us (level)
  no operation moved by 1% of the time
where the time goes in v9:
time: 90.1 us; the launch traced here: 89.7 us
  blocking collectives  33 us (37%)
  starting transfers between devices  25 us (28%)
  Pallas kernels  21.1 us (23%)
  waiting for transfers between devices  7.61 us (8%)
  other arithmetic  1.2 us (1%)
  local copies, waits for them, and re-layouts  1.05 us (1%)
    all_to_all x2, blocking collectives, total(): values = jnp.sum(lax.all_to_all(copies, axis, 0, 0, tiled=True), axis=0)  33 us
    ppermute x4, starting transfers between devices, shifted(): return lax.ppermute(value, AXES, pairs)  25 us
    ppermute x4, waiting for transfers between devices, shifted(): return lax.ppermute(value, AXES, pairs)  7.61 us
    pallas_call x1, Pallas kernels, far_pair(): call(far_pair_body, 'far_pair', (out, out), 6 * 10 ** 9)  5.71 us
    pallas_call x1, Pallas kernels, own_pair(): call(own_pair_body, 'own_pair', (out, out), 6 * 10 ** 9)  5.52 us
    pallas_call x1, Pallas kernels, first_pair(): call(first_pair_body, 'first_pair', (out, out), 6 * 10 ** 9)  5.52 us
    pallas_call x2, Pallas kernels, own_block(): call(body, 'own', shape(16, packed.shape[1]), 2 * 10 ** 9)  4.06 us
  transfers between devices with their start and end apart: 4, of which 1 were waited for; matrix products, arithmetic and copies ran while one was open for 0% of the time, Pallas kernels for 17%

profile of v9, /device:TPU:1, one launch (start us, length us, event | category | flops | bytes accessed | tf_op | source)
XLA Modules:
  0.0 89.7 jit_solution(6244006783129818671)
XLA Ops:
  0.6 0.0 copy-start
  0.6 0.8 constant_dynamic-update-slice_fusion.1
  1.5 0.1 copy-done
  1.6 0.0 copy-start.4
  1.6 4.8 %collective-permute-start.1 = (f32[24,1536]{1,0:T(8,128)S(1)}, f32[24,1536]{1,0:T(8,128)S(1)}, u32[]{:S(2)}, u32[]{:S(2)}) collective-permute-start(f32[24,1536]{1,0:T(8,128)S(1)} %constant_dynamic-update-slice_fusion.packed_ref.own_ref), channel_id=1, source_target_pairs={{0,2},{1,3},{2,4},{3,5},{4,6},{5,7},{6,8},{7,9},{8,10},{9,11},{10,... | collective-permute-start | bytes 442376 | tf_op jit(solution)/shard_map/ppermute | solution.py:182
  6.4 13.2 %collective-permute-start = (f32[24,1536]{1,0:T(8,128)S(1)}, f32[24,1536]{1,0:T(8,128)S(1)}, u32[]{:S(2)}, u32[]{:S(2)}) collective-permute-start(f32[24,1536]{1,0:T(8,128)S(1)} %constant_dynamic-update-slice_fusion.packed_ref.own_ref), channel_id=1, source_target_pairs={{0,1023},{1,0},{2,1},{3,2},{4,3},{5,4},{6,5},{7,6},{8,7},{9,8},{10... | collective-permute-start | bytes 442376 | tf_op jit(solution)/shard_map/ppermute | solution.py:182
  19.6 0.0 copy-done.4
  19.6 0.1 copy.21.inv_ref
  19.7 0.2 prepare.1
  19.9 1.5 %own.2.near_base_ref = f32[16,1536]{1,0:T(8,128)S(1)} custom-call(bf16[1536,64]{1,0:T(8,128)(2,1)S(1)} %get-tuple-element.11.left_ref, bf16[32,1536]{1,0:T(8,128)(2,1)S(1)} %get-tuple-element.12.sides_ref, f32[24,1536]{1,0:T(8,128)S(1)} %constant_dynamic-update-slice_fusion.packed_ref.own_ref, f32[8,1]{1,0:T(8,128)S(1)} %copy.21.inv_ref), custom_call_target="tpu_custom_call" | custom-call | flops 2000000000 | bytes 600000 | tf_op jit(solution)/shard_map/own/pallas_call | solution.py:176
  21.4 7.6 %collective-permute-done.1.far_ref.other_ref = f32[24,1536]{1,0:T(8,128)S(1)} collective-permute-done((f32[24,1536]{1,0:T(8,128)S(1)}, f32[24,1536]{1,0:T(8,128)S(1)}, u32[]{:S(2)}, u32[]{:S(2)}) %collective-permute-start.1) | collective-permute-done | bytes 147488 | tf_op jit(solution)/shard_map/ppermute | solution.py:182
  29.0 5.5 %first_pair.1 = (f32[16,1536]{1,0:T(8,128)S(1)}, f32[16,1536]{1,0:T(8,128)S(1)}) custom-call(bf16[1536,64]{1,0:T(8,128)(2,1)S(1)} %get-tuple-element.11.left_ref, bf16[32,1536]{1,0:T(8,128)(2,1)S(1)} %get-tuple-element.12.sides_ref, f32[24,1536]{1,0:T(8,128)S(1)} %collective-permute-done.1.far_ref.other_ref, f32[8,1]{1,0:T(8,128)S(1)} %copy.21.inv_ref, ...), custom_call_target="tpu_custom_call" | custom-call | flops 6000000000 | bytes 600000 | tf_op jit(solution)/shard_map/first_pair/pallas_call | solution.py:166
  34.5 0.0 collective-permute-done.one_ref.far_ref
  34.5 5.7 %far_pair.1 = (f32[16,1536]{1,0:T(8,128)S(1)}, f32[16,1536]{1,0:T(8,128)S(1)}) custom-call(f32[24,1536]{1,0:T(8,128)S(1)} %collective-permute-done.one_ref.far_ref, f32[24,1536]{1,0:T(8,128)S(1)} %collective-permute-done.1.far_ref.other_ref, f32[8,1]{1,0:T(8,128)S(1)} %copy.21.inv_ref, f32[16,1536]{1,0:T(8,128)S(1)} %get-tuple-element.13.base_ref), custom_call_target="tpu_custom_call" | custom-call | flops 6000000000 | bytes 600000 | tf_op jit(solution)/shard_map/far_pair/pallas_call | solution.py:171
  40.2 4.9 %collective-permute-start.2 = (f32[16,1536]{1,0:T(8,128)S(1)}, f32[16,1536]{1,0:T(8,128)S(1)}, u32[]{:S(2)}, u32[]{:S(2)}) collective-permute-start(f32[16,1536]{1,0:T(8,128)S(1)} %get-tuple-element.17), channel_id=1, source_target_pairs={{0,1022},{1,1023},{2,0},{3,1},{4,2},{5,3},{6,4},{7,5},{8,6},{9,7},... | collective-permute-start | bytes 294920 | tf_op jit(solution)/shard_map/ppermute | solution.py:182
  45.1 5.5 %own_pair.1 = (f32[16,1536]{1,0:T(8,128)S(1)}, f32[16,1536]{1,0:T(8,128)S(1)}) custom-call(bf16[1536,64]{1,0:T(8,128)(2,1)S(1)} %get-tuple-element.11.left_ref, bf16[32,1536]{1,0:T(8,128)(2,1)S(1)} %get-tuple-element.12.sides_ref, f32[24,1536]{1,0:T(8,128)S(1)} %collective-permute-done.one_ref.far_ref, f32[8,1]{1,0:T(8,128)S(1)} %copy.21.inv_ref, ...), custom_call_target="tpu_custom_call" | custom-call | flops 6000000000 | bytes 600000 | tf_op jit(solution)/shard_map/own_pair/pallas_call | solution.py:161
  50.7 0.0 copy-start.1
  50.7 2.1 %collective-permute-start.3 = (f32[16,1536]{1,0:T(8,128)S(1)}, f32[16,1536]{1,0:T(8,128)S(1)}, u32[]{:S(2)}, u32[]{:S(2)}) collective-permute-start(f32[16,1536]{1,0:T(8,128)S(1)} %get-tuple-element.18), channel_id=1, source_target_pairs={{0,1},{1,2},{2,3},{3,4},{4,5},{5,6},{6,7},{7,8},{8,9},{9,10},{10,1... | collective-permute-start | bytes 294920 | tf_op jit(solution)/shard_map/ppermute | solution.py:182
  52.8 0.0 collective-permute-done.2.refs_0_
  52.8 0.0 copy-start.3
  52.8 2.6 %own.3 = f32[16,1536]{1,0:T(8,128)S(1)} custom-call(bf16[1536,64]{1,0:T(8,128)(2,1)S(1)} %get-tuple-element.11.left_ref, bf16[32,1536]{1,0:T(8,128)(2,1)S(1)} %get-tuple-element.12.sides_ref, f32[24,1536]{1,0:T(8,128)S(1)} %constant_dynamic-update-slice_fusion.packed_ref.own_ref, f32[8,1]{1,0:T(8,128)S(1)} %copy.21.inv_ref, ...), custom_call_target="tpu_custom_call" | custom-call | flops 2000000000 | bytes 600000 | tf_op jit(solution)/shard_map/own/pallas_call | solution.py:176
  55.4 0.0 collective-permute-done.3
  55.4 0.0 copy-done.1
  55.4 0.0 copy-done.3
  55.4 0.2 multiply_reduce_fusion.3
  55.6 0.0 copy-start.2
  55.6 0.1 pad_maximum_fusion
  55.7 21.4 %all_to_all.12 = f32[32,1,64]{2,1,0:T(1,128)S(1)} all-to-all(f32[32,1,64]{2,1,0:T(1,128)S(1)} %broadcast_in_dim.7), channel_id=1, replica_groups=mesh['hi'=32,'lo'=32] {'lo'}, dimensions={0} | all-to-all | bytes 16384 | tf_op jit(solution)/shard_map/all_to_all | solution.py:189
  77.2 11.6 %all_to_all.13 = f32[32,1,64]{2,1,0:T(1,128)S(1)} all-to-all(f32[32,1,64]{2,1,0:T(1,128)S(1)} %broadcast_in_dim.8), channel_id=1, replica_groups=mesh['hi'=32,'lo'=32] {'hi'}, dimensions={0} | all-to-all | bytes 16384 | tf_op jit(solution)/shard_map/all_to_all | solution.py:189
  88.8 0.1 maximum_divide_fusion
  88.9 0.0 copy-done.2
  88.9 0.8 multiply_add_fusion
  (5 shorter events, 0.1 us)
Async XLA Ops:
  0.6 0.9 %copy-start = (f32[16,1536]{1,0:T(8,128)S(1)}, f32[16,1536]{1,0:T(8,128)}, u32[]{:S(2)}) copy-start(f32[16,1536]{1,0:T(8,128)} %param.11) | copy-start | bytes 294916
  1.6 18.0 %copy-start.4 = (f32[8]{0:T(128)S(1)}, f32[8]{0:T(128)}, u32[]{:S(2)}) copy-start(f32[8]{0:T(128)} %param.7) | copy-start | bytes 100
  1.6 27.4 %collective-permute-start.1 = (f32[24,1536]{1,0:T(8,128)S(1)}, f32[24,1536]{1,0:T(8,128)S(1)}, u32[]{:S(2)}, u32[]{:S(2)}) collective-permute-start(f32[24,1536]{1,0:T(8,128)S(1)} %constant_dynamic-update-slice_fusion.packed_ref.own_ref), channel_id=1, source_target_pairs={{0,2},{1,3},{2,4},{3,5},{4,6},{5,7},{6,8},{7,9},{8,10},{9,11},{10,... | collective-permute-start | bytes 442376 | tf_op jit(solution)/shard_map/ppermute | solution.py:182
  6.4 28.1 %collective-permute-start = (f32[24,1536]{1,0:T(8,128)S(1)}, f32[24,1536]{1,0:T(8,128)S(1)}, u32[]{:S(2)}, u32[]{:S(2)}) collective-permute-start(f32[24,1536]{1,0:T(8,128)S(1)} %constant_dynamic-update-slice_fusion.packed_ref.own_ref), channel_id=1, source_target_pairs={{0,1023},{1,0},{2,1},{3,2},{4,3},{5,4},{6,5},{7,6},{8,7},{9,8},{10... | collective-permute-start | bytes 442376 | tf_op jit(solution)/shard_map/ppermute | solution.py:182
  40.2 12.6 %collective-permute-start.2 = (f32[16,1536]{1,0:T(8,128)S(1)}, f32[16,1536]{1,0:T(8,128)S(1)}, u32[]{:S(2)}, u32[]{:S(2)}) collective-permute-start(f32[16,1536]{1,0:T(8,128)S(1)} %get-tuple-element.17), channel_id=1, source_target_pairs={{0,1022},{1,1023},{2,0},{3,1},{4,2},{5,3},{6,4},{7,5},{8,6},{9,7},... | collective-permute-start | bytes 294920 | tf_op jit(solution)/shard_map/ppermute | solution.py:182
  50.7 4.7 %copy-start.1 = (f32[16,1536]{1,0:T(8,128)S(1)}, f32[16,1536]{1,0:T(8,128)}, u32[]{:S(2)}) copy-start(f32[16,1536]{1,0:T(8,128)} %param.10) | copy-start | bytes 294916
  50.7 4.7 %collective-permute-start.3 = (f32[16,1536]{1,0:T(8,128)S(1)}, f32[16,1536]{1,0:T(8,128)S(1)}, u32[]{:S(2)}, u32[]{:S(2)}) collective-permute-start(f32[16,1536]{1,0:T(8,128)S(1)} %get-tuple-element.18), channel_id=1, source_target_pairs={{0,1},{1,2},{2,3},{3,4},{4,5},{5,6},{6,7},{7,8},{8,9},{9,10},{10,1... | collective-permute-start | bytes 294920 | tf_op jit(solution)/shard_map/ppermute | solution.py:182
  52.8 2.6 %copy-start.3 = (f32[1536]{0:T(1024)S(1)}, f32[1536]{0:T(1024)}, u32[]{:S(2)}) copy-start(f32[1536]{0:T(1024)} %param.8) | copy-start | bytes 18436
  55.6 33.3 %copy-start.2 = (f32[16,1536]{1,0:T(8,128)S(1)}, f32[16,1536]{1,0:T(8,128)}, u32[]{:S(2)}) copy-start(f32[16,1536]{1,0:T(8,128)} %param.9) | copy-start | bytes 294916

commit v10 on v9

--- a/solution.py
+++ b/solution.py
@@ -10,7 +10,7 @@
 
 ROUNDS = 3
 TILE = 256
-AXES = ("hi", "lo")
+AXES = ("hi", "ring", "core")
 VMEM_LIMIT = 40 * 1024 * 1024
 
 LN2 = math.log(2.0)
@@ -183,7 +183,7 @@
 
 
 def total(values):
-    for axis in ("lo", "hi"):
+    for axis in (("ring",), ("hi", "core")):
         count = lax.axis_size(axis)
         copies = jnp.broadcast_to(values[None], (count,) + values.shape)
         values = jnp.sum(lax.all_to_all(copies, axis, 0, 0, tiled=True), axis=0)
@@ -225,8 +225,7 @@
 
 def solution(mesh):
     devices = mesh.devices.reshape(-1)
-    low = 32
-    split = Mesh(devices.reshape(devices.size // low, low), AXES)
+    split = Mesh(devices.reshape(devices.size // 32, 16, 2), AXES)
     columns = P(None, AXES)
     return jax.shard_map(
         local,

time: 90.1 us -> 91.5 us (1.016)
  blocking collectives: 33 us -> 34.5 us
    all_to_all x2, blocking collectives: 33 us -> 34.5 us  [total(): values = jnp.sum(lax.all_to_all(copies, axis, 0, 0, tiled=True), axis=0)]
where the time goes in v10:
time: 91.5 us; the launch traced here: 91.2 us
  blocking collectives  34.5 us (38%)
  starting transfers between devices  25 us (27%)
  Pallas kernels  21.1 us (23%)
  waiting for transfers between devices  7.61 us (8%)
  other arithmetic  1.2 us (1%)
  local copies, waits for them, and re-layouts  1.06 us (1%)
    all_to_all x2, blocking collectives, total(): values = jnp.sum(lax.all_to_all(copies, axis, 0, 0, tiled=True), axis=0)  34.5 us
    ppermute x4, starting transfers between devices, shifted(): return lax.ppermute(value, AXES, pairs)  25 us
    ppermute x4, waiting for transfers between devices, shifted(): return lax.ppermute(value, AXES, pairs)  7.61 us
    pallas_call x1, Pallas kernels, far_pair(): call(far_pair_body, 'far_pair', (out, out), 6 * 10 ** 9)  5.71 us
    pallas_call x1, Pallas kernels, own_pair(): call(own_pair_body, 'own_pair', (out, out), 6 * 10 ** 9)  5.52 us
    pallas_call x1, Pallas kernels, first_pair(): call(first_pair_body, 'first_pair', (out, out), 6 * 10 ** 9)  5.52 us
    pallas_call x2, Pallas kernels, own_block(): call(body, 'own', shape(16, packed.shape[1]), 2 * 10 ** 9)  4.06 us
  transfers between devices with their start and end apart: 4, of which 1 were waited for; matrix products, arithmetic and copies ran while one was open for 0% of the time, Pallas kernels for 17%

profile of v10, /device:TPU:1, one launch (start us, length us, event | category | flops | bytes accessed | tf_op | source)
XLA Modules:
  0.0 91.2 jit_solution(16314733764543457667)
XLA Ops:
  0.6 0.0 copy-start
  0.6 0.8 constant_dynamic-update-slice_fusion.1
  1.5 0.1 copy-done
  1.6 0.0 copy-start.4
  1.6 4.8 %collective-permute-start.1 = (f32[24,1536]{1,0:T(8,128)S(1)}, f32[24,1536]{1,0:T(8,128)S(1)}, u32[]{:S(2)}, u32[]{:S(2)}) collective-permute-start(f32[24,1536]{1,0:T(8,128)S(1)} %constant_dynamic-update-slice_fusion.packed_ref.own_ref), channel_id=1, source_target_pairs={{0,2},{1,3},{2,4},{3,5},{4,6},{5,7},{6,8},{7,9},{8,10},{9,11},{10,... | collective-permute-start | bytes 442376 | tf_op jit(solution)/shard_map/ppermute | solution.py:182
  6.4 13.2 %collective-permute-start = (f32[24,1536]{1,0:T(8,128)S(1)}, f32[24,1536]{1,0:T(8,128)S(1)}, u32[]{:S(2)}, u32[]{:S(2)}) collective-permute-start(f32[24,1536]{1,0:T(8,128)S(1)} %constant_dynamic-update-slice_fusion.packed_ref.own_ref), channel_id=1, source_target_pairs={{0,1023},{1,0},{2,1},{3,2},{4,3},{5,4},{6,5},{7,6},{8,7},{9,8},{10... | collective-permute-start | bytes 442376 | tf_op jit(solution)/shard_map/ppermute | solution.py:182
  19.6 0.0 copy-done.4
  19.6 0.1 copy.21.inv_ref
  19.7 0.2 prepare.1
  19.9 1.5 %own.2.near_base_ref = f32[16,1536]{1,0:T(8,128)S(1)} custom-call(bf16[1536,64]{1,0:T(8,128)(2,1)S(1)} %get-tuple-element.11.left_ref, bf16[32,1536]{1,0:T(8,128)(2,1)S(1)} %get-tuple-element.12.sides_ref, f32[24,1536]{1,0:T(8,128)S(1)} %constant_dynamic-update-slice_fusion.packed_ref.own_ref, f32[8,1]{1,0:T(8,128)S(1)} %copy.21.inv_ref), custom_call_target="tpu_custom_call" | custom-call | flops 2000000000 | bytes 600000 | tf_op jit(solution)/shard_map/own/pallas_call | solution.py:176
  21.4 7.6 %collective-permute-done.1.far_ref.other_ref = f32[24,1536]{1,0:T(8,128)S(1)} collective-permute-done((f32[24,1536]{1,0:T(8,128)S(1)}, f32[24,1536]{1,0:T(8,128)S(1)}, u32[]{:S(2)}, u32[]{:S(2)}) %collective-permute-start.1) | collective-permute-done | bytes 147488 | tf_op jit(solution)/shard_map/ppermute | solution.py:182
  29.0 5.5 %first_pair.1 = (f32[16,1536]{1,0:T(8,128)S(1)}, f32[16,1536]{1,0:T(8,128)S(1)}) custom-call(bf16[1536,64]{1,0:T(8,128)(2,1)S(1)} %get-tuple-element.11.left_ref, bf16[32,1536]{1,0:T(8,128)(2,1)S(1)} %get-tuple-element.12.sides_ref, f32[24,1536]{1,0:T(8,128)S(1)} %collective-permute-done.1.far_ref.other_ref, f32[8,1]{1,0:T(8,128)S(1)} %copy.21.inv_ref, ...), custom_call_target="tpu_custom_call" | custom-call | flops 6000000000 | bytes 600000 | tf_op jit(solution)/shard_map/first_pair/pallas_call | solution.py:166
  34.5 0.0 collective-permute-done.one_ref.far_ref
  34.5 5.7 %far_pair.1 = (f32[16,1536]{1,0:T(8,128)S(1)}, f32[16,1536]{1,0:T(8,128)S(1)}) custom-call(f32[24,1536]{1,0:T(8,128)S(1)} %collective-permute-done.one_ref.far_ref, f32[24,1536]{1,0:T(8,128)S(1)} %collective-permute-done.1.far_ref.other_ref, f32[8,1]{1,0:T(8,128)S(1)} %copy.21.inv_ref, f32[16,1536]{1,0:T(8,128)S(1)} %get-tuple-element.13.base_ref), custom_call_target="tpu_custom_call" | custom-call | flops 6000000000 | bytes 600000 | tf_op jit(solution)/shard_map/far_pair/pallas_call | solution.py:171
  40.2 4.9 %collective-permute-start.2 = (f32[16,1536]{1,0:T(8,128)S(1)}, f32[16,1536]{1,0:T(8,128)S(1)}, u32[]{:S(2)}, u32[]{:S(2)}) collective-permute-start(f32[16,1536]{1,0:T(8,128)S(1)} %get-tuple-element.17), channel_id=1, source_target_pairs={{0,1022},{1,1023},{2,0},{3,1},{4,2},{5,3},{6,4},{7,5},{8,6},{9,7},... | collective-permute-start | bytes 294920 | tf_op jit(solution)/shard_map/ppermute | solution.py:182
  45.1 5.5 %own_pair.1 = (f32[16,1536]{1,0:T(8,128)S(1)}, f32[16,1536]{1,0:T(8,128)S(1)}) custom-call(bf16[1536,64]{1,0:T(8,128)(2,1)S(1)} %get-tuple-element.11.left_ref, bf16[32,1536]{1,0:T(8,128)(2,1)S(1)} %get-tuple-element.12.sides_ref, f32[24,1536]{1,0:T(8,128)S(1)} %collective-permute-done.one_ref.far_ref, f32[8,1]{1,0:T(8,128)S(1)} %copy.21.inv_ref, ...), custom_call_target="tpu_custom_call" | custom-call | flops 6000000000 | bytes 600000 | tf_op jit(solution)/shard_map/own_pair/pallas_call | solution.py:161
  50.7 0.0 copy-start.1
  50.7 2.1 %collective-permute-start.3 = (f32[16,1536]{1,0:T(8,128)S(1)}, f32[16,1536]{1,0:T(8,128)S(1)}, u32[]{:S(2)}, u32[]{:S(2)}) collective-permute-start(f32[16,1536]{1,0:T(8,128)S(1)} %get-tuple-element.18), channel_id=1, source_target_pairs={{0,1},{1,2},{2,3},{3,4},{4,5},{5,6},{6,7},{7,8},{8,9},{9,10},{10,1... | collective-permute-start | bytes 294920 | tf_op jit(solution)/shard_map/ppermute | solution.py:182
  52.8 0.0 collective-permute-done.2.refs_0_
  52.8 0.0 copy-start.3
  52.8 2.6 %own.3 = f32[16,1536]{1,0:T(8,128)S(1)} custom-call(bf16[1536,64]{1,0:T(8,128)(2,1)S(1)} %get-tuple-element.11.left_ref, bf16[32,1536]{1,0:T(8,128)(2,1)S(1)} %get-tuple-element.12.sides_ref, f32[24,1536]{1,0:T(8,128)S(1)} %constant_dynamic-update-slice_fusion.packed_ref.own_ref, f32[8,1]{1,0:T(8,128)S(1)} %copy.21.inv_ref, ...), custom_call_target="tpu_custom_call" | custom-call | flops 2000000000 | bytes 600000 | tf_op jit(solution)/shard_map/own/pallas_call | solution.py:176
  55.4 0.0 collective-permute-done.3
  55.4 0.0 copy-done.1
  55.4 0.0 copy-done.3
  55.4 0.2 multiply_reduce_fusion.3
  55.6 0.0 copy-start.2
  55.6 0.1 pad_maximum_fusion
  55.7 13.8 %all_to_all.12 = f32[16,1,64]{2,1,0:T(1,128)S(1)} all-to-all(f32[16,1,64]{2,1,0:T(1,128)S(1)} %broadcast_in_dim.7), channel_id=1, replica_groups=mesh['hi'=32,'ring'=16,'core'=2] {'ring'}, dimensions={0} | all-to-all | bytes 8192 | tf_op jit(solution)/shard_map/all_to_all | solution.py:189
  69.6 20.7 %all_to_all.13 = f32[64,1,64]{2,1,0:T(1,128)S(1)} all-to-all(f32[64,1,64]{2,1,0:T(1,128)S(1)} %broadcast_in_dim.8), channel_id=1, replica_groups=mesh['hi'=32,'ring'=16,'core'=2] {'hi','core'}, dimensions={0} | all-to-all | bytes 32768 | tf_op jit(solution)/shard_map/all_to_all | solution.py:189
  90.3 0.1 maximum_divide_fusion
  90.4 0.0 copy-done.2
  90.4 0.8 multiply_add_fusion
  (5 shorter events, 0.1 us)
Async XLA Ops:
  0.6 0.9 %copy-start = (f32[16,1536]{1,0:T(8,128)S(1)}, f32[16,1536]{1,0:T(8,128)}, u32[]{:S(2)}) copy-start(f32[16,1536]{1,0:T(8,128)} %param.11) | copy-start | bytes 294916
  1.6 18.0 %copy-start.4 = (f32[8]{0:T(128)S(1)}, f32[8]{0:T(128)}, u32[]{:S(2)}) copy-start(f32[8]{0:T(128)} %param.7) | copy-start | bytes 100
  1.6 27.4 %collective-permute-start.1 = (f32[24,1536]{1,0:T(8,128)S(1)}, f32[24,1536]{1,0:T(8,128)S(1)}, u32[]{:S(2)}, u32[]{:S(2)}) collective-permute-start(f32[24,1536]{1,0:T(8,128)S(1)} %constant_dynamic-update-slice_fusion.packed_ref.own_ref), channel_id=1, source_target_pairs={{0,2},{1,3},{2,4},{3,5},{4,6},{5,7},{6,8},{7,9},{8,10},{9,11},{10,... | collective-permute-start | bytes 442376 | tf_op jit(solution)/shard_map/ppermute | solution.py:182
  6.4 28.1 %collective-permute-start = (f32[24,1536]{1,0:T(8,128)S(1)}, f32[24,1536]{1,0:T(8,128)S(1)}, u32[]{:S(2)}, u32[]{:S(2)}) collective-permute-start(f32[24,1536]{1,0:T(8,128)S(1)} %constant_dynamic-update-slice_fusion.packed_ref.own_ref), channel_id=1, source_target_pairs={{0,1023},{1,0},{2,1},{3,2},{4,3},{5,4},{6,5},{7,6},{8,7},{9,8},{10... | collective-permute-start | bytes 442376 | tf_op jit(solution)/shard_map/ppermute | solution.py:182
  40.2 12.6 %collective-permute-start.2 = (f32[16,1536]{1,0:T(8,128)S(1)}, f32[16,1536]{1,0:T(8,128)S(1)}, u32[]{:S(2)}, u32[]{:S(2)}) collective-permute-start(f32[16,1536]{1,0:T(8,128)S(1)} %get-tuple-element.17), channel_id=1, source_target_pairs={{0,1022},{1,1023},{2,0},{3,1},{4,2},{5,3},{6,4},{7,5},{8,6},{9,7},... | collective-permute-start | bytes 294920 | tf_op jit(solution)/shard_map/ppermute | solution.py:182
  50.7 4.7 %copy-start.1 = (f32[16,1536]{1,0:T(8,128)S(1)}, f32[16,1536]{1,0:T(8,128)}, u32[]{:S(2)}) copy-start(f32[16,1536]{1,0:T(8,128)} %param.10) | copy-start | bytes 294916
  50.7 4.7 %collective-permute-start.3 = (f32[16,1536]{1,0:T(8,128)S(1)}, f32[16,1536]{1,0:T(8,128)S(1)}, u32[]{:S(2)}, u32[]{:S(2)}) collective-permute-start(f32[16,1536]{1,0:T(8,128)S(1)} %get-tuple-element.18), channel_id=1, source_target_pairs={{0,1},{1,2},{2,3},{3,4},{4,5},{5,6},{6,7},{7,8},{8,9},{9,10},{10,1... | collective-permute-start | bytes 294920 | tf_op jit(solution)/shard_map/ppermute | solution.py:182
  52.8 2.6 %copy-start.3 = (f32[1536]{0:T(1024)S(1)}, f32[1536]{0:T(1024)}, u32[]{:S(2)}) copy-start(f32[1536]{0:T(1024)} %param.8) | copy-start | bytes 18436
  55.6 34.8 %copy-start.2 = (f32[16,1536]{1,0:T(8,128)S(1)}, f32[16,1536]{1,0:T(8,128)}, u32[]{:S(2)}) copy-start(f32[16,1536]{1,0:T(8,128)} %param.9) | copy-start | bytes 294916
